TPU v7x, 256 devices: a whole 4x4x8 slice. The times are simulated.
256 devices in a mesh: region: 8 (over x, core), dom: 32 (over y, z).
Axes of the slice: x: 4, y: 4, z: 8, core: 2. Of those that a mesh axis runs over, the one named last changes fastest.
Arguments:
- params: float32 [59, 262144], P(None, ('region', 'dom')), may hold values from -6.4 to 6.4, as said below
- first_moment: float32 [59, 262144], P(None, ('region', 'dom')), may hold values from -0.3 to 0.3
- second_moment: float32 [59, 262144], P(None, ('region', 'dom')), may hold values from 0.0001 to 0.01
- piece_blocks: int32 [256, 32, 2], P(('region', 'dom')), may hold values from 0 to 9, all different within a row
- piece_live: int32 [256, 32], P(('region', 'dom')), may hold values from 1 to 2
- piece_owner: int32 [256, 32], P(('region', 'dom')), may hold values from 0 to 31, as said below
- piece_cell: int32 [256, 32], P(('region', 'dom')), may hold values from 0 to 63, as said below
- target: float32 [256, 8, 3, 256], P(('region', 'dom')), may hold values from 0 to 1
- background: float32 [3], replicated, may hold values from 0 to 1
Outputs:
- gradient: float32 [59, 262144], P(None, ('region', 'dom'))
- new_params: float32 [59, 262144], P(None, ('region', 'dom'))
- new_first: float32 [59, 262144], P(None, ('region', 'dom'))
- new_second: float32 [59, 262144], P(None, ('region', 'dom'))
Inputs may be any that keep to these rules, and one draw needn't show every extreme that they name: `params`: rows 0 to 2: z in [2, 4], x / z and y / z in [-1.6, 1.6]; rows 3 to 5 in [-0.9, 0.2]; row 6 in [0.5, 1.5]; rows 7 to 9 in [-1, 1]; row 10 in [-5.5, -1.8]; rows 11 to 58 in [-2, 2]. `piece_blocks`: the entries of one list are different pool blocks. `piece_owner`: each part sends at most 2 pieces to one owner; in every region some owner receives exactly 2 pieces from every part. `piece_cell`: the pieces that one owner receives have different cells.
All inputs are finite; a program needn't handle non-finite values.
Results may differ from a plain program's by a relative error of at most 0.0003.
Values sent between devices are 32-bit elements; how exact they have to be, the bound alone decides.
A program may use at most 64 MiB of HBM per device.

v0:
```python
import jax
import jax.numpy as jnp
from jax import lax
from jax.sharding import PartitionSpec as P

PARAMS = 59
TSIDE = 16
WIN = 8
BLOCK = 128
MAXD = 8
PIECES = 32
PIX = 256
TILE_DEV = 8
CELLS = 64


harmonic_zero = 0.28209479177387814
harmonic_one = 0.4886025119029199
harmonic_two = (
    1.0925484305920792,
    -1.0925484305920792,
    0.31539156525252005,
    -1.0925484305920792,
    0.5462742152960396,
)
harmonic_three = (
    -0.5900435899266435,
    2.890611442640554,
    -0.4570457994644658,
    0.3731763325901154,
    -0.4570457994644658,
    1.445305721320277,
    -0.5900435899266435,
)
beta_one = 0.9
beta_two = 0.999
rate = 0.001
adam_step = 100
tiny = 1e-08
group_pieces = 8


def extended(block, sides, width):
    for axis, dim in sides:
        count = lax.axis_size(axis)
        forward = [(i, i + 1) for i in range(count - 1)]
        backward = [(target, source) for source, target in forward]
        low = lax.ppermute(
            lax.slice_in_dim(block, block.shape[dim] - width, None, axis=dim), axis, forward
        )
        high = lax.ppermute(lax.slice_in_dim(block, 0, width, axis=dim), axis, backward)
        block = jnp.concatenate([low, block, high], axis=dim)
    return block


def splat_table(block, screen_px):
    mean_x, mean_y, mean_z = (block[0], block[1], block[2])
    scales = jnp.exp(block[3:6])
    quat_raw = block[6:10]
    quat_norm = quat_raw / jnp.sqrt(jnp.sum(quat_raw * quat_raw, axis=0))
    quat_w, quat_x, quat_y, quat_z = (quat_norm[0], quat_norm[1], quat_norm[2], quat_norm[3])
    rotation = [
        [
            1 - 2 * (quat_y * quat_y + quat_z * quat_z),
            2 * (quat_x * quat_y - quat_w * quat_z),
            2 * (quat_x * quat_z + quat_w * quat_y),
        ],
        [
            2 * (quat_x * quat_y + quat_w * quat_z),
            1 - 2 * (quat_x * quat_x + quat_z * quat_z),
            2 * (quat_y * quat_z - quat_w * quat_x),
        ],
        [
            2 * (quat_x * quat_z - quat_w * quat_y),
            2 * (quat_y * quat_z + quat_w * quat_x),
            1 - 2 * (quat_x * quat_x + quat_y * quat_y),
        ],
    ]
    focal_px = 0.3125 * screen_px
    inv_z = 1.0 / mean_z
    jac_rows = [
        [focal_px * inv_z, 0.0 * inv_z, -focal_px * mean_x * inv_z * inv_z],
        [0.0 * inv_z, focal_px * inv_z, -focal_px * mean_y * inv_z * inv_z],
    ]
    projected = []
    for out_row in range(2):
        entries = []
        for out_col in range(3):
            acc_term = jac_rows[out_row][0] * rotation[0][out_col]
            acc_term = acc_term + jac_rows[out_row][1] * rotation[1][out_col]
            acc_term = acc_term + jac_rows[out_row][2] * rotation[2][out_col]
            entries.append(acc_term * scales[out_col])
        projected.append(entries)
    sigma_xx = (
        projected[0][0] * projected[0][0]
        + projected[0][1] * projected[0][1]
        + projected[0][2] * projected[0][2]
        + 0.3
    )
    sigma_xy = (
        projected[0][0] * projected[1][0]
        + projected[0][1] * projected[1][1]
        + projected[0][2] * projected[1][2]
    )
    sigma_yy = (
        projected[1][0] * projected[1][0]
        + projected[1][1] * projected[1][1]
        + projected[1][2] * projected[1][2]
        + 0.3
    )
    determinant = sigma_xx * sigma_yy - sigma_xy * sigma_xy
    conic_xx = sigma_yy / determinant
    conic_xy = -sigma_xy / determinant
    conic_yy = sigma_xx / determinant
    centre_u = 0.5 * screen_px + focal_px * mean_x * inv_z
    centre_v = 0.5 * screen_px + focal_px * mean_y * inv_z
    opacity = jax.nn.sigmoid(block[10])
    length = jnp.sqrt(mean_x * mean_x + mean_y * mean_y + mean_z * mean_z)
    dir_x, dir_y, dir_z = (mean_x / length, mean_y / length, mean_z / length)
    sq_x, sq_y, sq_z = (dir_x * dir_x, dir_y * dir_y, dir_z * dir_z)
    harmonics = [
        harmonic_zero + 0.0 * dir_x,
        -harmonic_one * dir_y,
        harmonic_one * dir_z,
        -harmonic_one * dir_x,
        harmonic_two[0] * dir_x * dir_y,
        harmonic_two[1] * dir_y * dir_z,
        harmonic_two[2] * (2 * sq_z - sq_x - sq_y),
        harmonic_two[3] * dir_x * dir_z,
        harmonic_two[4] * (sq_x - sq_y),
        harmonic_three[0] * dir_y * (3 * sq_x - sq_y),
        harmonic_three[1] * dir_x * dir_y * dir_z,
        harmonic_three[2] * dir_y * (4 * sq_z - sq_x - sq_y),
        harmonic_three[3] * dir_z * (2 * sq_z - 3 * sq_x - 3 * sq_y),
        harmonic_three[4] * dir_x * (4 * sq_z - sq_x - sq_y),
        harmonic_three[5] * dir_z * (sq_x - sq_y),
        harmonic_three[6] * dir_x * (sq_x - 3 * sq_y),
    ]
    basis = jnp.stack(harmonics, axis=0)
    coeffs = block[11:59].reshape(3, 16, block.shape[1])
    colour = jnp.maximum(jnp.sum(coeffs * basis[None], axis=1) + 0.5, 0.0)
    return jnp.stack(
        [
            centre_u,
            centre_v,
            conic_xx,
            conic_xy,
            conic_yy,
            opacity,
            colour[0],
            colour[1],
            colour[2],
        ],
        axis=0,
    )


def render_piece(chosen, slot_flags, tile_index):
    pixels = jnp.arange(TSIDE * TSIDE, dtype=jnp.int32)
    column = tile_index % WIN
    tile_row = tile_index // WIN
    pixel_x = (TSIDE * column + pixels % TSIDE).astype(chosen.dtype) + 0.5
    pixel_y = (TSIDE * tile_row + pixels // TSIDE).astype(chosen.dtype) + 0.5
    carry_log = jnp.zeros((TSIDE * TSIDE,), chosen.dtype)
    colour_sum = jnp.zeros((3, TSIDE * TSIDE), chosen.dtype)
    for slot_no in range(chosen.shape[1]):
        terms = chosen[:, slot_no]
        centre_u, centre_v, conic_xx, conic_xy, conic_yy, opacity = (
            terms[0],
            terms[1],
            terms[2],
            terms[3],
            terms[4],
            terms[5],
        )
        colour = terms[6:9]
        offset_x = pixel_x[None, :] - centre_u[:, None]
        offset_y = pixel_y[None, :] - centre_v[:, None]
        quadratic = (
            conic_xx[:, None] * offset_x * offset_x
            + 2.0 * conic_xy[:, None] * offset_x * offset_y
            + conic_yy[:, None] * offset_y * offset_y
        )
        alphas = (opacity * slot_flags[slot_no])[:, None] * jnp.exp(-0.5 * quadratic)
        log_keep = jnp.log1p(-alphas)
        before = carry_log[None, :] + jnp.cumsum(log_keep, axis=0) - log_keep
        weight = alphas * jnp.exp(before)
        colour_sum = colour_sum + jnp.dot(colour, weight, precision=lax.Precision.HIGHEST)
        carry_log = carry_log + jnp.sum(log_keep, axis=0)
    return jnp.concatenate([colour_sum, jnp.exp(carry_log)[None, :]], axis=0)


def render_listed(terms, present, blocks_row, live_row, tile_index):
    chosen = terms[:, blocks_row]
    slot_ids = jnp.arange(blocks_row.shape[0], dtype=jnp.int32)
    slot_flags = present[blocks_row] * (slot_ids < live_row).astype(present.dtype)
    return render_piece(chosen, slot_flags, tile_index)


def composite_grads(cell_grid, target_tiles, background):
    cell_grid = cell_grid.reshape(TILE_DEV, MAXD, 4, PIX)
    colours = cell_grid[:, :, :3]
    transmit = 1.0 - cell_grid[:, :, 3]
    in_front = jnp.ones((TILE_DEV, PIX), jnp.float32)
    composite = jnp.zeros((TILE_DEV, 3, PIX), jnp.float32)
    fronts = []
    for depth_slot in range(MAXD):
        fronts.append(in_front)
        composite = composite + in_front[:, None, :] * colours[:, depth_slot]
        in_front = in_front * transmit[:, depth_slot]
    composite = composite + in_front[:, None, :] * background[:, None]
    residual = composite - target_tiles
    behind = jnp.broadcast_to(background[None, :, None], (TILE_DEV, 3, PIX))
    cell_grads = [None] * MAXD
    for depth_slot in reversed(range(MAXD)):
        grad_trans = fronts[depth_slot] * jnp.sum(residual * behind, axis=1)
        grad_colour = fronts[depth_slot][:, None, :] * residual
        cell_grads[depth_slot] = jnp.concatenate([grad_colour, grad_trans[:, None, :]], axis=1)
        behind = colours[:, depth_slot] + transmit[:, depth_slot][:, None, :] * behind
    return jnp.stack(cell_grads, axis=1).reshape(CELLS, 4 * PIX)


def on_device(
    params,
    first_moment,
    second_moment,
    piece_blocks,
    piece_live,
    piece_owner,
    piece_cell,
    target,
    background,
):
    region_idx = lax.axis_index("region")
    regions = lax.axis_size("region")
    own_blocks = params.shape[1] // BLOCK
    screen_px = float(WIN * TSIDE)
    present = jnp.concatenate(
        [
            (region_idx > 0).astype(jnp.float32)[None],
            jnp.ones((own_blocks,), jnp.float32),
            (region_idx < regions - 1).astype(jnp.float32)[None],
        ]
    )

    def masked_terms(columns):
        terms = splat_table(columns, screen_px).reshape(9, own_blocks + 2, BLOCK)
        return jnp.where(present[None, :, None] > 0, terms, jnp.zeros_like(terms))

    pool_cols = extended(params, (("region", 1),), BLOCK)
    pool_terms, terms_pull = jax.vjp(masked_terms, pool_cols)
    group_count = PIECES // group_pieces
    grouped_blocks = piece_blocks[0].reshape(group_count, group_pieces, piece_blocks.shape[2])
    grouped_live = piece_live[0].reshape(group_count, group_pieces)
    grouped_tiles = jnp.arange(PIECES, dtype=jnp.int32).reshape(group_count, group_pieces)

    def render_group(terms, group_blocks, group_live, group_tiles):
        return jax.vmap(render_listed, in_axes=(None, None, 0, 0, 0))(
            terms, present, group_blocks, group_live, group_tiles
        )

    def forward_group(items):
        return render_group(pool_terms, items[0], items[1], items[2])

    rendered = lax.map(forward_group, (grouped_blocks, grouped_live, grouped_tiles)).reshape(
        PIECES, 4, PIX
    )
    outbound = jnp.concatenate([rendered[:, :3], 1.0 - rendered[:, 3:]], axis=1).reshape(
        PIECES, 4 * PIX
    )
    doms = lax.axis_size("dom")
    my_dom = lax.axis_index("dom")
    cell_range = jnp.arange(CELLS, dtype=jnp.int32)
    all_owner, all_cell = (
        lax.all_gather(piece_owner, "dom", axis=0, tiled=True),
        lax.all_gather(piece_cell, "dom", axis=0, tiled=True),
    )
    all_owner = all_owner.reshape(doms * PIECES)
    all_cell = all_cell.reshape(doms * PIECES)

    def select_rows():
        mine = all_owner == my_dom
        return (mine[:, None] & (all_cell[:, None] == cell_range[None, :])).astype(jnp.float32)

    onehot = select_rows()
    cell_grid = jnp.zeros((CELLS, 4 * PIX), jnp.float32) + jnp.dot(
        onehot.T,
        lax.all_gather(outbound, "dom", axis=0, tiled=True),
        precision=lax.Precision.HIGHEST,
    )
    grid_grads = composite_grads(cell_grid, target[0], background)
    onehot = select_rows()
    piece_grads = lax.psum_scatter(
        jnp.dot(onehot, grid_grads, precision=lax.Precision.HIGHEST),
        "dom",
        scatter_dimension=0,
        tiled=True,
    )
    cotangent = piece_grads.reshape(group_count, group_pieces, 4, PIX)

    def backward_group(running, items):
        group_blocks, group_live, group_tiles, group_cot = items
        _, pull_back = jax.vjp(
            lambda terms: render_group(terms, group_blocks, group_live, group_tiles), pool_terms
        )
        return (running + pull_back(group_cot)[0], None)

    term_grads, _ = lax.scan(
        backward_group,
        jnp.zeros_like(pool_terms),
        (grouped_blocks, grouped_live, grouped_tiles, cotangent),
    )
    inner_zero = jnp.zeros((PARAMS, (own_blocks - 2) * BLOCK), jnp.float32)
    pool_grads = terms_pull(term_grads)[0]
    rims = jnp.concatenate([pool_grads[:, :BLOCK], pool_grads[:, -BLOCK:]], axis=1)
    crossed = extended(rims, (("region", 1),), BLOCK)
    incoming = jnp.concatenate([crossed[:, :BLOCK], inner_zero, crossed[:, 3 * BLOCK :]], axis=1)
    gradient = pool_grads[:, BLOCK:-BLOCK] + incoming
    new_first = beta_one * first_moment + (1 - beta_one) * gradient
    new_second = beta_two * second_moment + (1 - beta_two) * gradient * gradient
    update = (
        new_first
        / (1 - beta_one**adam_step)
        / (jnp.sqrt(new_second / (1 - beta_two**adam_step)) + tiny)
    )
    new_params = params - rate * update
    return (gradient, new_params, new_first, new_second)


def solution(mesh):
    in_specs = (
        P(None, ("region", "dom")),
        P(None, ("region", "dom")),
        P(None, ("region", "dom")),
        P(("region", "dom"), None, None),
        P(("region", "dom"), None),
        P(("region", "dom"), None),
        P(("region", "dom"), None),
        P(("region", "dom"), None, None, None),
        P(),
    )
    out_specs = (
        P(None, ("region", "dom")),
        P(None, ("region", "dom")),
        P(None, ("region", "dom")),
        P(None, ("region", "dom")),
    )
    return jax.shard_map(
        on_device, mesh=mesh, in_specs=in_specs, out_specs=out_specs, check_vma=False
    )
```

profile of v0, /device:TPU:1, one launch (start us, length us, event | category | flops | bytes accessed | tf_op | source)
XLA Modules:
  0.0 518.5 jit_solution(11689469629901024946)
XLA Ops:
  8.0 5.1 collective-permute-start.1
  19.9 46.0 %while.26 = (s32[]{:T(128)}, f32[4,8,4,256]{3,2,1,0:T(4,128)S(1)}, s32[4,8,2]{1,2,0:T(2,128)S(1)}, f32[9,10,128]{2,0,1:T(8,128)S(1)}, s32[4,8]{1,0:T(4,128)S(1)}...) while((s32[]{:T(128)}, f32[4,8,4,256]{3,2,1,0:T(4,128)S(1)}, s32[4,8,2]{1,2,0:T(2,128)S(1)}, ...), condition=%wide.region_7.8_spmd, body=%wide.region_2.7_spmd.sunk | while | flops 107774232 | bytes 5277265 | solution.py:265
  66.8 34.4 %all-gather = s32[32,1,32]{2,1,0:T(1,128)S(1)} all-gather(s32[1,1,32]{2,1,0:T(1,128)S(1)} %bitcast.557), channel_id=1, replica_groups=mesh['region'=8,'dom'=32] {'dom'}, dimensions={0}, use_global_device_ids=true | all-gather | bytes 4224 | tf_op jit(solution)/shard_map/all_gather | solution.py:275
  101.4 29.5 %all-gather.1 = s32[32,1,32]{2,1,0:T(1,128)S(1)} all-gather(s32[1,1,32]{2,1,0:T(1,128)S(1)} %bitcast.558), channel_id=1, replica_groups=mesh['region'=8,'dom'=32] {'dom'}, dimensions={0}, use_global_device_ids=true | all-gather | bytes 4224 | tf_op jit(solution)/shard_map/all_gather | solution.py:276
  131.7 16.3 %all-gather.4.cloned.1.call-done = f32[1024,1024]{1,0:T(8,128)} async-done(((f32[32,1024]{1,0:T(8,128)}), f32[1024,1024]{1,0:T(8,128)}) %all-gather.4.cloned.1.call-update) | async-done | bytes 4194320 | tf_op jit(solution)/shard_map/all_gather | solution.py:288
  147.9 4.1 fusion.116
  152.8 3.8 fusion.114
  156.7 216.1 %reduce-scatter.2.cloned.1.call-done = f32[32,1024]{1,0:T(8,128)} async-done(((f32[1024,1024]{1,0:T(8,128)}), f32[32,1024]{1,0:T(8,128)}) %reduce-scatter.2.cloned.1.call-update) | async-done | bytes 131088 | tf_op jit(solution)/shard_map/reduce_scatter | solution.py:293
  372.8 122.7 %while.27 = (s32[]{:T(128)}, f32[9,10,128]{2,0,1:T(8,128)S(1)}, s32[4,8,2]{1,2,0:T(2,128)S(1)}, f32[4,8,4,256]{3,1,2,0:T(8,128)}, f32[9,10,128]{2,0,1:T(8,128)S(...) while((s32[]{:T(128)}, f32[9,10,128]{2,0,1:T(8,128)S(1)}, ...), condition=%wide.region_38.39_spmd, body=%wide.region_17.38_spmd.sunk | while | flops 220889376 | bytes 28468952 | solution.py:308
  379.7 4.1 fusion.246
  389.4 2.7 fusion.248
  394.7 7.2 %fusion.252 = (f32[8,128]{1,0:T(8,128)S(1)}, f32[8,128]{1,0:T(8,128)S(1)}, f32[8,128]{1,0:T(8,128)S(1)}, f32[8,128]{1,0:T(8,128)S(1)}, f32[8,128]{1,0:T(8,128)S(...) fusion(f32[8,128]{1,0:T(8,128)S(1)} %bitcast.514, ...), kind=kLoop, calls=%fused_computation.122.clone.1 | loop fusion | flops 25415680 | bytes 7479296 | tf_op jit(solution)/shard_map/while/body/eval_jaxpr/transpose(jvp(vmap()))/reduce_sum | solution.py:182
  410.4 4.1 fusion.246
  420.1 2.7 fusion.248
  425.3 7.2 %fusion.252 = (f32[8,128]{1,0:T(8,128)S(1)}, f32[8,128]{1,0:T(8,128)S(1)}, f32[8,128]{1,0:T(8,128)S(1)}, f32[8,128]{1,0:T(8,128)S(1)}, f32[8,128]{1,0:T(8,128)S(...) fusion(f32[8,128]{1,0:T(8,128)S(1)} %bitcast.514, ...), kind=kLoop, calls=%fused_computation.122.clone.1 | loop fusion | flops 25415680 | bytes 7479296 | tf_op jit(solution)/shard_map/while/body/eval_jaxpr/transpose(jvp(vmap()))/reduce_sum | solution.py:182
  441.1 4.1 fusion.246
  448.2 2.5 fusion.251
  450.8 2.7 fusion.248
  456.0 7.2 %fusion.252 = (f32[8,128]{1,0:T(8,128)S(1)}, f32[8,128]{1,0:T(8,128)S(1)}, f32[8,128]{1,0:T(8,128)S(1)}, f32[8,128]{1,0:T(8,128)S(1)}, f32[8,128]{1,0:T(8,128)S(...) fusion(f32[8,128]{1,0:T(8,128)S(1)} %bitcast.514, ...), kind=kLoop, calls=%fused_computation.122.clone.1 | loop fusion | flops 25415680 | bytes 7479296 | tf_op jit(solution)/shard_map/while/body/eval_jaxpr/transpose(jvp(vmap()))/reduce_sum | solution.py:182
  471.8 4.1 fusion.246
  481.4 2.7 fusion.248
  486.7 7.2 %fusion.252 = (f32[8,128]{1,0:T(8,128)S(1)}, f32[8,128]{1,0:T(8,128)S(1)}, f32[8,128]{1,0:T(8,128)S(1)}, f32[8,128]{1,0:T(8,128)S(1)}, f32[8,128]{1,0:T(8,128)S(...) fusion(f32[8,128]{1,0:T(8,128)S(1)} %bitcast.514, ...), kind=kLoop, calls=%fused_computation.122.clone.1 | loop fusion | flops 25415680 | bytes 7479296 | tf_op jit(solution)/shard_map/while/body/eval_jaxpr/transpose(jvp(vmap()))/reduce_sum | solution.py:182
  496.9 8.5 %collective-permute-start.2 = (f32[59,128]{1,0:T(8,128)S(1)}, f32[59,128]{1,0:T(8,128)S(1)}, u32[]{:S(2)}, u32[]{:S(2)}) collective-permute-start(f32[59,128]{1,0:T(8,128)S(1)} %get-tuple-element.554), channel_id=1, source_target_pairs={{0,32},{32,64},{64,96},{96,128},{128,160},{160,192},{192,224},{1,3... | collective-permute-start | bytes 90632 | tf_op jit(solution)/shard_map/ppermute | solution.py:48
  507.4 3.2 collective-permute-done.3
  (445 shorter events, 122.7 us)
Async XLA Ops:
  7.2 140.8 %all-gather.4.cloned.1.call-start = ((), (), s32[]{:S(2)}) async-start(), calls=%async_computation.1 | async-start | bytes 4325376 | tf_op jit(solution)/shard_map/all_gather | solution.py:288
  8.0 10.9 %collective-permute-start.1 = (f32[59,128]{1,0:T(8,128)S(1)}, f32[59,128]{1,0:T(8,128)S(1)}, u32[]{:S(2)}, u32[]{:S(2)}) collective-permute-start(f32[59,128]{1,0:T(8,128)S(1)} %get-tuple-element.564), channel_id=1, source_target_pairs={{32,0},{64,32},{96,64},{128,96},{160,128},{192,160},{224,192},{33,... | collective-permute-start | bytes 90632 | tf_op jit(solution)/shard_map/ppermute | solution.py:51
  13.1 4.7 collective-permute-start
  19.9 46.9 %copy-start.5 = (s32[1,32]{1,0:T(1,128)S(1)}, s32[1,32]{1,0:T(1,128)}, u32[]{:S(2)}) copy-start(s32[1,32]{1,0:T(1,128)} %param.18) | copy-start | bytes 388
  19.9 81.5 %copy-start.6 = (s32[1,32]{1,0:T(1,128)S(1)}, s32[1,32]{1,0:T(1,128)}, u32[]{:S(2)}) copy-start(s32[1,32]{1,0:T(1,128)} %param.19) | copy-start | bytes 388
  65.9 86.3 %copy-start.4 = (f32[3]{0:T(128)S(1)}, f32[3]{0:T(128)}, u32[]{:S(2)}) copy-start(f32[3]{0:T(128)} %param.21) | copy-start | bytes 40
  65.9 86.4 %copy-start.3 = (f32[1,8,3,256]{3,1,2,0:T(8,128)S(1)}, f32[1,8,3,256]{3,1,2,0:T(8,128)}, u32[]{:S(2)}) copy-start(f32[1,8,3,256]{3,1,2,0:T(8,128)} %param.20) | copy-start | bytes 73732
  66.8 306.0 %reduce-scatter.2.cloned.1.call-start = ((), (), s32[]{:S(2)}) async-start(), calls=%async_computation.2 | async-start | bytes 4325376 | tf_op jit(solution)/shard_map/reduce_scatter | solution.py:293
  372.8 137.8 %copy-start = (f32[59,1024]{1,0:T(8,128)S(1)}, f32[59,1024]{1,0:T(8,128)}, u32[]{:S(2)}) copy-start(f32[59,1024]{1,0:T(8,128)} %param.13) | copy-start | bytes 724996
  372.8 137.8 %copy-start.1 = (f32[59,1024]{1,0:T(8,128)S(1)}, f32[59,1024]{1,0:T(8,128)}, u32[]{:S(2)}) copy-start(f32[59,1024]{1,0:T(8,128)} %param.14) | copy-start | bytes 724996
  372.8 137.8 %copy-start.2 = (f32[59,1024]{1,0:T(8,128)S(1)}, f32[59,1024]{1,0:T(8,128)}, u32[]{:S(2)}) copy-start(f32[59,1024]{1,0:T(8,128)} %param.15) | copy-start | bytes 724996
  496.9 10.5 %collective-permute-start.2 = (f32[59,128]{1,0:T(8,128)S(1)}, f32[59,128]{1,0:T(8,128)S(1)}, u32[]{:S(2)}, u32[]{:S(2)}) collective-permute-start(f32[59,128]{1,0:T(8,128)S(1)} %get-tuple-element.554), channel_id=1, source_target_pairs={{0,32},{32,64},{64,96},{96,128},{128,160},{160,192},{192,224},{1,3... | collective-permute-start | bytes 90632 | tf_op jit(solution)/shard_map/ppermute | solution.py:48
  505.4 5.2 %collective-permute-start.3 = (f32[59,128]{1,0:T(8,128)S(1)}, f32[59,128]{1,0:T(8,128)S(1)}, u32[]{:S(2)}, u32[]{:S(2)}) collective-permute-start(f32[59,128]{1,0:T(8,128)S(1)} %get-tuple-element.555), channel_id=1, source_target_pairs={{32,0},{64,32},{96,64},{128,96},{160,128},{192,160},{224,192},{33,... | collective-permute-start | bytes 90632 | tf_op jit(solution)/shard_map/ppermute | solution.py:51
Sparse Core Ops, SparseCore 0:
  66.9 81.0 all-gather.3
  156.8 215.9 reduce-scatter.1
where the time goes:
time: 519 us
  waiting for transfers between devices  236 us (45%)
  other arithmetic  98 us (19%)
  blocking collectives  63.9 us (12%)
  matrix products  60.6 us (12%)
  local copies, waits for them, and re-layouts  26.6 us (5%)
  starting transfers between devices  17.5 us (3%)
  between operations  14.6 us (3%)
    reduce_scatter x1, waiting for transfers between devices, on_device(): lax.psum_scatter(jnp.dot(onehot, grid_grads, precision=lax.Precision.HIGH...  216 us
    dot_general x24, matrix products, render_piece(): jnp.dot(colour, weight, precision=lax.Precision.HIGHEST)  52.7 us
    another operation x24, other arithmetic, render_piece(): before = carry_log[None, :] + jnp.cumsum(log_keep, axis=0) - log_keep  42.2 us
    all_gather x1, blocking collectives, on_device(): lax.all_gather(piece_owner, 'dom', axis=0, tiled=True)  34.4 us
    all_gather x1, blocking collectives, on_device(): lax.all_gather(piece_cell, 'dom', axis=0, tiled=True)  29.5 us
    reduce_sum x4, other arithmetic, render_piece(): conic_yy[:, None] * offset_y * offset_y  28.9 us
    all_gather x1, waiting for transfers between devices, on_device(): lax.all_gather(outbound, 'dom', axis=0, tiled=True)  16.3 us
    ppermute x2, starting transfers between devices, extended(): lax.ppermute(lax.slice_in_dim(block, block.shape[dim] - width, None, axis...  10.4 us
  transfers between devices with their start and end apart: 6, of which 3 were waited for; matrix products, arithmetic and copies ran while one was open for 1% of the time, Pallas kernels for 0%

commit v1 on v0

v1 whole, which is shorter than its diff:
```python
import math

import jax
import jax.numpy as jnp
import ml_dtypes
import numpy as np
from jax import lax
from jax.experimental import pallas as pl
from jax.experimental.pallas import tpu as pltpu
from jax.sharding import PartitionSpec as P

PARAMS = 59
TSIDE = 16
WIN = 8
BLOCK = 128
BLOCKS = 8
MAXD = 8
PIECES = 32
PIX = 256
TILE_DEV = 8
CELLS = 64
POOL = 10
SLOTS = 2
SUB = 8
STEPS = BLOCK // SUB
TAB = POOL + 1
PLANES = 16
ROWS = 64
ORIGIN_X = 64.0
ORIGIN_Y = 32.0

harmonic_zero = 0.28209479177387814
harmonic_one = 0.4886025119029199
harmonic_two = (
    1.0925484305920792,
    -1.0925484305920792,
    0.31539156525252005,
    -1.0925484305920792,
    0.5462742152960396,
)
harmonic_three = (
    -0.5900435899266435,
    2.890611442640554,
    -0.4570457994644658,
    0.3731763325901154,
    -0.4570457994644658,
    1.445305721320277,
    -0.5900435899266435,
)
beta_one = 0.9
beta_two = 0.999
rate = 0.001
adam_step = 100
tiny = 1e-08

f32 = jnp.float32
bf16 = jnp.bfloat16
MESH = pl.DeviceIdType.MESH
VMEM_LIMIT = 48 * 1024 * 1024


def pixel_monomials():
    bf = ml_dtypes.bfloat16
    tile = np.arange(PIECES)[:, None]
    pixel = np.arange(PIX)[None, :]
    x = (TSIDE * (tile % WIN) + pixel % TSIDE + 0.5 - ORIGIN_X).astype(np.float32)
    y = (TSIDE * (tile // WIN) + pixel // TSIDE + 0.5 - ORIGIN_Y).astype(np.float32)

    def two(value):
        head = value.astype(bf).astype(np.float32)
        return [head, value - head]

    return [np.ones_like(x), x, y] + two(x * x) + two(x * y) + two(y * y)


def exponent_features():
    rows = [row for row in pixel_monomials() for _ in range(3)]
    rows += [np.zeros_like(rows[0])] * (32 - len(rows))
    return np.stack(rows, axis=1).astype(ml_dtypes.bfloat16)


def moment_features():
    rows = pixel_monomials()
    rows += [np.zeros_like(rows[0])] * (16 - len(rows))
    return np.stack(rows, axis=1).astype(ml_dtypes.bfloat16)


def split(value, parts):
    out = []
    rest = value
    for part in range(parts):
        head = rest.astype(bf16)
        out.append(head)
        if part < parts - 1:
            rest = rest - head.astype(f32)
    return out


def exact_pick(onehot, value):
    picks = onehot.astype(bf16)
    total = None
    for part in reversed(split(value, 3)):
        term = jnp.dot(picks, part, preferred_element_type=f32)
        total = term if total is None else total + term
    return total


def iota(shape, dim):
    return lax.broadcasted_iota(jnp.int32, shape, dim)


def to_column(row):
    n = row.shape[1]
    spread = jnp.broadcast_to(row, (n, n))
    return jnp.sum(jnp.where(iota((n, n), 0) == iota((n, n), 1), spread, 0.0), axis=1, keepdims=True)


def to_row(column):
    n = column.shape[0]
    spread = jnp.broadcast_to(column, (n, n))
    return jnp.sum(jnp.where(iota((n, n), 0) == iota((n, n), 1), spread, 0.0), axis=0, keepdims=True)


def geometry(mean_x, mean_y, mean_z, log_a, log_b, log_c, quat_w, quat_x, quat_y, quat_z):
    screen_px = float(WIN * TSIDE)
    scales = (jnp.exp(log_a), jnp.exp(log_b), jnp.exp(log_c))
    norm = 1.0 / jnp.sqrt(quat_w * quat_w + quat_x * quat_x + quat_y * quat_y + quat_z * quat_z)
    quat_w, quat_x, quat_y, quat_z = quat_w * norm, quat_x * norm, quat_y * norm, quat_z * norm
    rotation = [
        [
            1 - 2 * (quat_y * quat_y + quat_z * quat_z),
            2 * (quat_x * quat_y - quat_w * quat_z),
            2 * (quat_x * quat_z + quat_w * quat_y),
        ],
        [
            2 * (quat_x * quat_y + quat_w * quat_z),
            1 - 2 * (quat_x * quat_x + quat_z * quat_z),
            2 * (quat_y * quat_z - quat_w * quat_x),
        ],
        [
            2 * (quat_x * quat_z - quat_w * quat_y),
            2 * (quat_y * quat_z + quat_w * quat_x),
            1 - 2 * (quat_x * quat_x + quat_y * quat_y),
        ],
    ]
    focal_px = 0.3125 * screen_px
    inv_z = 1.0 / mean_z
    ratio_x, ratio_y = mean_x * inv_z, mean_y * inv_z
    focal_z = focal_px * inv_z
    rows = []
    for ratio, axis in ((ratio_x, 0), (ratio_y, 1)):
        rows.append(
            [
                focal_z * (rotation[axis][col] - ratio * rotation[2][col]) * scales[col]
                for col in range(3)
            ]
        )
    sigma_xx = rows[0][0] * rows[0][0] + rows[0][1] * rows[0][1] + rows[0][2] * rows[0][2] + 0.3
    sigma_xy = rows[0][0] * rows[1][0] + rows[0][1] * rows[1][1] + rows[0][2] * rows[1][2]
    sigma_yy = rows[1][0] * rows[1][0] + rows[1][1] * rows[1][1] + rows[1][2] * rows[1][2] + 0.3
    inv_det = 1.0 / (sigma_xx * sigma_yy - sigma_xy * sigma_xy)
    return (
        focal_px * ratio_x + (0.5 * screen_px - ORIGIN_X),
        focal_px * ratio_y + (0.5 * screen_px - ORIGIN_Y),
        sigma_yy * inv_det,
        -sigma_xy * inv_det,
        sigma_xx * inv_det,
    )


def harmonics(mean_x, mean_y, mean_z):
    inv_length = 1.0 / jnp.sqrt(mean_x * mean_x + mean_y * mean_y + mean_z * mean_z)
    dir_x, dir_y, dir_z = mean_x * inv_length, mean_y * inv_length, mean_z * inv_length
    sq_x, sq_y, sq_z = dir_x * dir_x, dir_y * dir_y, dir_z * dir_z
    return (
        -harmonic_one * dir_y,
        harmonic_one * dir_z,
        -harmonic_one * dir_x,
        harmonic_two[0] * dir_x * dir_y,
        harmonic_two[1] * dir_y * dir_z,
        harmonic_two[2] * (2 * sq_z - sq_x - sq_y),
        harmonic_two[3] * dir_x * dir_z,
        harmonic_two[4] * (sq_x - sq_y),
        harmonic_three[0] * dir_y * (3 * sq_x - sq_y),
        harmonic_three[1] * dir_x * dir_y * dir_z,
        harmonic_three[2] * dir_y * (4 * sq_z - sq_x - sq_y),
        harmonic_three[3] * dir_z * (2 * sq_z - 3 * sq_x - 3 * sq_y),
        harmonic_three[4] * dir_x * (4 * sq_z - sq_x - sq_y),
        harmonic_three[5] * dir_z * (sq_x - sq_y),
        harmonic_three[6] * dir_x * (sq_x - 3 * sq_y),
    )


def fill_pool(pool, params_ref, low_ref, high_ref):
    for b in range(PLANES):
        if b == 0 or b >= POOL:
            block = low_ref[...]
        elif b == POOL - 1:
            block = high_ref[...]
        else:
            block = params_ref[:, (b - 1) * BLOCK : b * BLOCK]
        pool[b * ROWS : b * ROWS + PARAMS, :] = block


def plane(ref, row):
    return ref[pl.ds(row, PLANES, stride=ROWS), :]


def put_plane(ref, row, value):
    ref[pl.ds(row, PLANES, stride=ROWS), :] = value


def raw_colour(pool, basis, colour):
    total = harmonic_zero * plane(pool, 11 + 16 * colour) + 0.5
    for k in range(1, 16):
        total = total + plane(pool, 11 + 16 * colour + k) * basis[k - 1]
    return total


def scan_forward(table, features, block):
    return jnp.dot(table[block], features, preferred_element_type=f32)


def roll_rows(value, shift):
    return pltpu.roll(value, shift % SUB, axis=0)


def forward_kernel(
    blocks_ref,
    live_ref,
    params_ref,
    low_ref,
    high_ref,
    features_ref,
    pieces_ref,
    table_ref,
    colour_table_ref,
    prefix_ref,
    segment_ref,
    pool,
    stage,
    turned,
    spread,
):
    fill_pool(pool, params_ref, low_ref, high_ref)
    region = lax.axis_index("region")
    regions = lax.axis_size("region")
    block_no = iota((PLANES, BLOCK), 0)
    present = (block_no > 0) & (block_no < POOL - 1)
    present = present | ((block_no == 0) & (region > 0))
    present = present | ((block_no == POOL - 1) & (region < regions - 1))

    means = [plane(pool, r) for r in range(3)]
    centre_u, centre_v, conic_xx, conic_xy, conic_yy = geometry(
        *means, *[plane(pool, r) for r in range(3, 10)]
    )
    opacity = 1.0 / (1.0 + jnp.exp(-plane(pool, 10)))
    log2_e = 1.0 / math.log(2.0)
    slope_x = conic_xx * centre_u + conic_xy * centre_v
    slope_y = conic_xy * centre_u + conic_yy * centre_v
    constant = jnp.log(opacity) - 0.5 * (centre_u * slope_x + centre_v * slope_y)
    constant = jnp.where(present, log2_e * constant, -1e30)
    terms = [
        constant,
        log2_e * slope_x,
        log2_e * slope_y,
        (-0.5 * log2_e) * conic_xx,
        (-log2_e) * conic_xy,
        (-0.5 * log2_e) * conic_yy,
    ]
    row = 0
    for term, copies in zip(terms, (1, 1, 1, 2, 2, 2)):
        parts = [part.astype(f32) for part in split(term, 3)]
        for _ in range(copies):
            for part in parts:
                put_plane(stage, row, part)
                row += 1
    for spare in range(row, ROWS):
        put_plane(stage, spare, jnp.zeros((PLANES, BLOCK), f32))
    basis = harmonics(*means)
    for c in range(3):
        put_plane(stage, 32 + c, jnp.maximum(raw_colour(pool, basis, c), 0.0))

    def turn(b, carry):
        rows = stage[pl.ds(pl.multiple_of(b * ROWS, ROWS), ROWS), :]
        turned[:, :ROWS] = rows.T
        ordered = jnp.concatenate(
            [turned[pl.ds(t, SUB, stride=STEPS), :ROWS] for t in range(STEPS)], axis=0
        )
        table_ref[b] = ordered[:, :32].astype(bf16)
        wide = []
        for c in range(3):
            column = ordered[:, 32 + c : 33 + c]
            spread[b, c] = jnp.broadcast_to(column, (BLOCK, BLOCK))
            wide.append([part for part in split(column, 3)])
        lane = iota((BLOCK, 64), 1)
        order = (0, 0, 0, 1, 1, 2)
        columns = jnp.zeros((BLOCK, 64), f32)
        for group, part in enumerate(order):
            for c in range(3):
                columns = jnp.where(
                    lane == group * 8 + c, jnp.broadcast_to(wide[c][part].astype(f32), (BLOCK, 64)), columns
                )
        colour_table_ref[b] = columns.astype(bf16)
        return carry

    lax.fori_loop(0, POOL, turn, 0)
    lane = iota((BLOCK, 32), 1)
    table_ref[POOL] = jnp.where(lane == 0, -1e30, 0.0).astype(bf16)
    colour_table_ref[POOL] = jnp.zeros((BLOCK, 64), bf16)
    spread[POOL] = jnp.zeros((3, BLOCK, BLOCK), f32)

    sub = iota((SUB, PIX), 0)

    def piece(p, carry):
        first = blocks_ref[p, 0]
        second = jnp.where(live_ref[0, p] > 1, blocks_ref[p, 1], POOL)
        features = features_ref[p]
        before = None
        colours = [None] * 3
        for j, block in enumerate((first, second)):
            exponent = scan_forward(table_ref, features, block)
            transmit = jnp.ones((SUB, PIX), f32)
            sums = [jnp.zeros((SUB, PIX), f32) for _ in range(3)]
            for t in range(STEPS):
                rows = slice(t * SUB, (t + 1) * SUB)
                weight = jnp.exp2(exponent[rows]) * transmit
                transmit = transmit - weight
                for c in range(3):
                    tone = spread[block, c, rows, :]
                    sums[c] = sums[c] + jnp.concatenate([tone, tone], axis=1) * weight
            run = transmit
            for shift in (1, 2, 4):
                run = run * jnp.where(sub >= shift, roll_rows(run, shift), 1.0)
            prefix = jnp.where(sub >= 1, roll_rows(run, 1), 1.0)
            total = run[SUB - 1 :, :]
            if before is not None:
                prefix = prefix * before
                total = total * before
            before = total
            prefix_ref[p, j] = prefix
            for c in range(3):
                piece_sum = prefix * sums[c]
                segment_ref[p, j, c] = piece_sum
                colours[c] = piece_sum if j == 0 else colours[c] + piece_sum
        for c in range(3):
            pieces_ref[pl.ds(p, 1), c * PIX : (c + 1) * PIX] = jnp.sum(
                colours[c], axis=0, keepdims=True
            )
        pieces_ref[pl.ds(p, 1), 3 * PIX :] = 1.0 - before
        return carry

    lax.fori_loop(0, PIECES, piece, 0)


def whole(memory=pltpu.VMEM):
    return pl.BlockSpec(memory_space=memory)


def render(blocks, live, params, low, high, features):
    shape = jax.ShapeDtypeStruct
    return pl.pallas_call(
        forward_kernel,
        out_shape=(
            shape((PIECES, 4 * PIX), f32),
            shape((TAB, BLOCK, 32), bf16),
            shape((TAB, BLOCK, 64), bf16),
            shape((PIECES, 2, SUB, PIX), f32),
            shape((PIECES, 2, 3, SUB, PIX), f32),
        ),
        in_specs=[whole(pltpu.SMEM)] * 2 + [whole()] * 4,
        out_specs=(whole(),) * 5,
        scratch_shapes=[
            pltpu.VMEM((PLANES * ROWS, BLOCK), f32),
            pltpu.VMEM((PLANES * ROWS, BLOCK), f32),
            pltpu.VMEM((BLOCK, BLOCK), f32),
            pltpu.VMEM((TAB, 3, BLOCK, BLOCK), f32),
        ],
        compiler_params=pltpu.CompilerParams(vmem_limit_bytes=VMEM_LIMIT),
        name="render_forward",
    )(blocks, live, params, low, high, features)


def backward_kernel(
    blocks_ref,
    live_ref,
    cotangent_ref,
    params_ref,
    low_ref,
    high_ref,
    features_ref,
    moments_ref,
    table_ref,
    colour_table_ref,
    prefix_ref,
    segment_ref,
    own_ref,
    edge_low_ref,
    edge_high_ref,
    pool,
    stage,
    turned,
    sums,
):
    sums[...] = jnp.zeros_like(sums)
    sub = iota((SUB, PIX), 0)
    nothing = jnp.zeros((16, PIX), bf16)

    def piece(p, carry):
        first = blocks_ref[p, 0]
        second = jnp.where(live_ref[0, p] > 1, blocks_ref[p, 1], POOL)
        features = features_ref[p]
        monomials = moments_ref[p]
        cot = jnp.concatenate(
            [
                cotangent_ref[pl.ds(pl.multiple_of(half * PIECES * SUB + p * SUB, SUB), SUB), :]
                for half in range(2)
            ],
            axis=1,
        )
        heads = [part.astype(f32) for part in split(cot, 3)]
        tones = jnp.concatenate([heads[0], heads[1], heads[2], heads[0], heads[1], heads[0]] + [jnp.zeros((16, PIX), f32)], axis=0)
        tones = tones.astype(bf16)
        colour_rows = jnp.concatenate([heads[0], heads[1]], axis=0).astype(bf16)
        for_gradient = jnp.concatenate([monomials, nothing], axis=0)
        for_weight = jnp.concatenate([nothing, colour_rows], axis=0)
        state = []
        for j, block in enumerate((first, second)):
            exponent = scan_forward(table_ref, features, block)
            tone = scan_forward(colour_table_ref, tones, block)
            transmit = prefix_ref[p, j]
            alphas, weights = [], []
            for t in range(STEPS):
                alpha = jnp.exp2(exponent[t * SUB : (t + 1) * SUB])
                weight = alpha * transmit
                transmit = transmit - weight
                alphas.append(alpha)
                weights.append(weight)
            seen = segment_ref[p, j, 0] * cot[0:1]
            for c in (1, 2):
                seen = seen + segment_ref[p, j, c] * cot[c : c + 1]
            run = seen
            for shift in (1, 2, 4):
                run = run + jnp.where(sub < SUB - shift, roll_rows(run, -shift), 0.0)
            state.append((block, tone, transmit, alphas, weights, run))
        behind = state[1][2][SUB - 1 :, :] * cot[3:4]
        for j in (1, 0):
            block, tone, transmit, alphas, weights, run = state[j]
            after = jnp.where(sub < SUB - 1, roll_rows(run, -1), 0.0) + behind
            behind = behind + run[0:1]
            ahead = after / transmit
            gradients = [None] * STEPS
            for t in reversed(range(STEPS)):
                gap = tone[t * SUB : (t + 1) * SUB] - ahead
                gradients[t] = weights[t] * gap
                ahead = ahead + alphas[t] * gap
            total = None
            for values, rows in ((gradients, for_gradient), (weights, for_weight)):
                for part in split(jnp.concatenate(values, axis=0), 2):
                    term = lax.dot_general(
                        part, rows, (((1,), (1,)), ((), ())), preferred_element_type=f32
                    )
                    total = term if total is None else total + term
            sums[block] = sums[block] + total
        return carry

    lax.fori_loop(0, PIECES, piece, 0)

    def turn(b, carry):
        for t in range(STEPS):
            turned[pl.ds(t, SUB, stride=STEPS), :32] = sums[b, t * SUB : (t + 1) * SUB, :]
        stage[pl.ds(pl.multiple_of(b * ROWS, ROWS), 32), :] = turned[:, :32].T
        return carry

    lax.fori_loop(0, POOL, turn, 0)
    for b in range(POOL, PLANES):
        stage[b * ROWS : b * ROWS + 32, :] = jnp.zeros((32, BLOCK), f32)

    fill_pool(pool, params_ref, low_ref, high_ref)
    means = [plane(pool, r) for r in range(3)]
    (centre_u, centre_v, conic_xx, conic_xy, conic_yy), geometry_pull = jax.vjp(
        geometry, *means, *[plane(pool, r) for r in range(3, 10)]
    )
    basis, harmonics_pull = jax.vjp(harmonics, *means)
    opacity = 1.0 / (1.0 + jnp.exp(-plane(pool, 10)))

    total = plane(stage, 0)
    sum_x, sum_y = plane(stage, 1), plane(stage, 2)
    sum_xx = plane(stage, 3) + plane(stage, 4)
    sum_xy = plane(stage, 5) + plane(stage, 6)
    sum_yy = plane(stage, 7) + plane(stage, 8)
    off_x = sum_x - centre_u * total
    off_y = sum_y - centre_v * total
    grad_xx = -0.5 * (sum_xx - centre_u * (sum_x + off_x))
    grad_xy = -(sum_xy - centre_u * sum_y - centre_v * off_x)
    grad_yy = -0.5 * (sum_yy - centre_v * (sum_y + off_y))
    grad_u = conic_xx * off_x + conic_xy * off_y
    grad_v = conic_xy * off_x + conic_yy * off_y
    grads = geometry_pull((grad_u, grad_v, grad_xx, grad_xy, grad_yy))
    tone_grads = []
    for c in range(3):
        grad = plane(stage, 16 + c) + plane(stage, 24 + c)
        raw = raw_colour(pool, basis, c)
        tone_grads.append(jnp.where(raw > 0, grad, jnp.where(raw == 0, 0.5 * grad, 0.0)))
    basis_grads = []
    for k in range(1, 16):
        basis_grads.append(
            sum(tone_grads[c] * plane(pool, 11 + 16 * c + k) for c in range(3))
        )
    mean_grads = harmonics_pull(tuple(basis_grads))
    for r in range(10):
        put_plane(stage, r, grads[r] + mean_grads[r] if r < 3 else grads[r])
    put_plane(stage, 10, total * (1.0 - opacity))
    for c in range(3):
        put_plane(stage, 11 + 16 * c, tone_grads[c] * harmonic_zero)
        for k in range(1, 16):
            put_plane(stage, 11 + 16 * c + k, tone_grads[c] * basis[k - 1])
    for b in range(POOL):
        block = stage[b * ROWS : b * ROWS + PARAMS, :]
        if b == 0:
            edge_low_ref[...] = block
        elif b == POOL - 1:
            edge_high_ref[...] = block
        else:
            own_ref[:, (b - 1) * BLOCK : b * BLOCK] = block


def pull(blocks, live, cotangent, params, low, high, features, moments, tables):
    shape = jax.ShapeDtypeStruct
    return pl.pallas_call(
        backward_kernel,
        out_shape=(
            shape((PARAMS, BLOCKS * BLOCK), f32),
            shape((PARAMS, BLOCK), f32),
            shape((PARAMS, BLOCK), f32),
        ),
        in_specs=[whole(pltpu.SMEM)] * 2 + [whole()] * 10,
        out_specs=(whole(),) * 3,
        scratch_shapes=[
            pltpu.VMEM((PLANES * ROWS, BLOCK), f32),
            pltpu.VMEM((PLANES * ROWS, BLOCK), f32),
            pltpu.VMEM((BLOCK, BLOCK), f32),
            pltpu.VMEM((TAB, BLOCK, 32), f32),
        ],
        compiler_params=pltpu.CompilerParams(vmem_limit_bytes=VMEM_LIMIT),
        name="render_backward",
    )(blocks, live, cotangent, params, low, high, features, moments, *tables)


def swap_kernel(right_cols, left_cols, right_src, left_src, from_left, from_right, send_sem, recv_sem):
    count = lax.axis_size("region")
    me = lax.axis_index("region")
    right, left = lax.rem(me + 1, count), lax.rem(me + count - 1, count)
    barrier = pltpu.get_barrier_semaphore()
    for other in (left, right):
        pl.semaphore_signal(barrier, inc=1, device_id={"region": other}, device_id_type=MESH)
    pl.semaphore_wait(barrier, 2)
    copies = []
    for k, (src, cols, dst, other) in enumerate(
        ((right_src, right_cols, from_left, right), (left_src, left_cols, from_right, left))
    ):
        copies.append(
            pltpu.make_async_remote_copy(
                src_ref=src.at[:, pl.ds(cols, BLOCK)],
                dst_ref=dst,
                send_sem=send_sem.at[k],
                recv_sem=recv_sem.at[k],
                device_id={"region": other},
                device_id_type=MESH,
            )
        )
    for copy in copies:
        copy.start()
    for copy in copies:
        copy.wait()


def swap(right_src, right_cols, left_src, left_cols, collective_id, name):
    def body(*refs):
        swap_kernel(right_cols, left_cols, *refs)

    return pl.pallas_call(
        body,
        out_shape=(jax.ShapeDtypeStruct((PARAMS, BLOCK), f32),) * 2,
        in_specs=[whole(pl.ANY)] * 2,
        out_specs=(whole(),) * 2,
        scratch_shapes=[pltpu.SemaphoreType.DMA((2,)), pltpu.SemaphoreType.DMA((2,))],
        compiler_params=pltpu.CompilerParams(collective_id=collective_id, has_side_effects=True),
        name=name,
    )(right_src, left_src)


def put_slots(ref, values):
    for k in range(SLOTS):
        for r in range(SUB):
            ref[pl.ds(k * SUB + r, 32, stride=SLOTS * SUB), :] = values[
                k * 32 : (k + 1) * 32, r * BLOCK : (r + 1) * BLOCK
            ]


def get_slots(ref):
    return jnp.concatenate(
        [
            jnp.concatenate(
                [ref[pl.ds(k * SUB + r, 32, stride=SLOTS * SUB), :] for r in range(SUB)], axis=1
            )
            for k in range(SLOTS)
        ],
        axis=0,
    )


def exchange_kernel(
    pieces_ref,
    owner_ref,
    cell_ref,
    target_ref,
    background_ref,
    out_ref,
    sent,
    got,
    labels,
    got_labels,
    replies,
    answers,
    send_sem,
    recv_sem,
    label_send,
    label_recv,
    reply_send,
    reply_recv,
):
    count = lax.axis_size("dom")
    me = lax.axis_index("dom")
    barrier = pltpu.get_barrier_semaphore()

    def greet(d, carry):
        pl.semaphore_signal(
            barrier, inc=1, device_id={"dom": lax.rem(me + d, count)}, device_id_type=MESH
        )
        return carry

    lax.fori_loop(1, count, greet, 0)

    owner_row = owner_ref[...].astype(f32)
    owner_col = to_column(owner_row)
    far_row = owner_row - me.astype(f32)
    far_row = jnp.where(far_row < 0, far_row + float(PIECES), far_row)
    far_col = to_column(far_row)
    same = jnp.broadcast_to(owner_row, (PIECES, PIECES)) == jnp.broadcast_to(owner_col, (PIECES, PIECES))
    first, second = iota((PIECES, PIECES), 0), iota((PIECES, PIECES), 1)
    rank_row = jnp.sum(jnp.where(same & (first < second), 1.0, 0.0), axis=0, keepdims=True)
    rank_col = jnp.sum(jnp.where(same & (second < first), 1.0, 0.0), axis=1, keepdims=True)
    slot_row = rank_row * 32.0 + far_row
    slot_col = rank_col * 32.0 + far_col
    slots = SLOTS * 32
    pack = jnp.broadcast_to(slot_row, (slots, PIECES)) == iota((slots, PIECES), 0).astype(f32)
    pack = jnp.where(pack, 1.0, 0.0)
    unpack = jnp.broadcast_to(slot_col, (PIECES, slots)) == iota((PIECES, slots), 1).astype(f32)
    unpack = jnp.where(unpack, 1.0, 0.0)
    cell_row = cell_ref[...].astype(f32) + 1.0
    label_col = jnp.sum(pack * cell_row, axis=1, keepdims=True) - 1.0

    put_slots(sent, exact_pick(pack, pieces_ref[...]))
    lane = iota((32, BLOCK), 1)
    label_rows = jnp.where(lane == 0, label_col[:32], jnp.where(lane == 1, label_col[32:], -1.0))
    for d in range(32):
        labels[d] = label_rows[d : d + 1]

    pl.semaphore_wait(barrier, count - 1)

    def payload(d):
        rows = pl.ds(pl.multiple_of(d * SLOTS * SUB, SLOTS * SUB), SLOTS * SUB)
        return pltpu.make_async_remote_copy(
            src_ref=sent.at[rows],
            dst_ref=got.at[rows],
            send_sem=send_sem.at[d],
            recv_sem=recv_sem.at[d],
            device_id={"dom": lax.rem(me + d, count)},
            device_id_type=MESH,
        )

    def label(d):
        return pltpu.make_async_remote_copy(
            src_ref=labels.at[d],
            dst_ref=got_labels.at[d],
            send_sem=label_send.at[d],
            recv_sem=label_recv.at[d],
            device_id={"dom": lax.rem(me + d, count)},
            device_id_type=MESH,
        )

    def reply(d):
        rows = pl.ds(pl.multiple_of(d * SLOTS * SUB, SLOTS * SUB), SLOTS * SUB)
        return pltpu.make_async_remote_copy(
            src_ref=replies.at[rows],
            dst_ref=answers.at[rows],
            send_sem=reply_send.at[d],
            recv_sem=reply_recv.at[d],
            device_id={"dom": lax.rem(me + count - d, count)},
            device_id_type=MESH,
        )

    def start_out(d, carry):
        payload(d).start()
        label(d).start()
        return carry

    def wait_out(d, carry):
        payload(d).wait()
        label(d).wait()
        return carry

    lax.fori_loop(1, count, start_out, 0)
    got[: SLOTS * SUB] = sent[: SLOTS * SUB]
    got_labels[0] = labels[0]
    lax.fori_loop(1, count, wait_out, 0)

    arrived = jnp.concatenate([got_labels[d] for d in range(32)], axis=0)
    arrived_col = jnp.concatenate([arrived[:, 0:1], arrived[:, 1:2]], axis=0)
    arrived_row = to_row(arrived_col)

    def cell_of(place):
        return ((place % TILE_DEV) * MAXD + place // TILE_DEV).astype(f32)

    gather = jnp.broadcast_to(arrived_row, (CELLS, slots)) == cell_of(iota((CELLS, slots), 0))
    gather = jnp.where(gather, 1.0, 0.0)
    scatter = jnp.broadcast_to(arrived_col, (slots, CELLS)) == cell_of(iota((slots, CELLS), 1))
    scatter = jnp.where(scatter, 1.0, 0.0)
    grid = exact_pick(gather, get_slots(got))

    def at(depth, channel):
        return grid[depth * SUB : (depth + 1) * SUB, channel * PIX : (channel + 1) * PIX]

    in_front = jnp.ones((TILE_DEV, PIX), f32)
    composite = [jnp.zeros((TILE_DEV, PIX), f32) for _ in range(3)]
    fronts = []
    for depth in range(MAXD):
        fronts.append(in_front)
        composite = [composite[c] + in_front * at(depth, c) for c in range(3)]
        in_front = in_front * (1.0 - at(depth, 3))
    residual = [
        composite[c] + in_front * background_ref[c] - target_ref[0, :, c, :] for c in range(3)
    ]
    behind = [jnp.full((TILE_DEV, PIX), background_ref[c], f32) for c in range(3)]
    rows = [None] * MAXD
    for depth in reversed(range(MAXD)):
        seen = residual[0] * behind[0] + residual[1] * behind[1] + residual[2] * behind[2]
        rows[depth] = jnp.concatenate(
            [fronts[depth] * residual[c] for c in range(3)] + [fronts[depth] * seen], axis=1
        )
        through = 1.0 - at(depth, 3)
        behind = [at(depth, c) + through * behind[c] for c in range(3)]
    put_slots(replies, exact_pick(scatter, jnp.concatenate(rows, axis=0)))

    def start_back(d, carry):
        reply(d).start()
        return carry

    def wait_back(d, carry):
        reply(d).wait()
        return carry

    lax.fori_loop(1, count, start_back, 0)
    answers[: SLOTS * SUB] = replies[: SLOTS * SUB]
    lax.fori_loop(1, count, wait_back, 0)

    cotangent = exact_pick(unpack, get_slots(answers))
    for half in range(2):
        for c in range(SUB):
            lanes = slice(c * PIX + half * BLOCK, c * PIX + (half + 1) * BLOCK)
            rows = cotangent[:, lanes] if c < 4 else jnp.zeros((PIECES, BLOCK), f32)
            out_ref[pl.ds(half * PIECES * SUB + c, PIECES, stride=SUB), :] = rows


def exchange(pieces, owner, cell, target, background):
    slots = pltpu.VMEM((32 * SLOTS * SUB, BLOCK), f32)
    label = pltpu.VMEM((32, 1, BLOCK), f32)
    return pl.pallas_call(
        exchange_kernel,
        out_shape=jax.ShapeDtypeStruct((2 * PIECES * SUB, BLOCK), f32),
        in_specs=[whole()] * 4 + [whole(pltpu.SMEM)],
        out_specs=whole(),
        scratch_shapes=[slots, slots, label, label, slots, slots]
        + [pltpu.SemaphoreType.DMA((32,))] * 6,
        compiler_params=pltpu.CompilerParams(
            collective_id=1, has_side_effects=True, vmem_limit_bytes=VMEM_LIMIT
        ),
        name="tiles_to_owners",
    )(pieces, owner, cell, target, background)


def adam_kernel(
    own_ref, from_left_ref, from_right_ref, params_ref, first_ref, second_ref,
    gradient_ref, new_params_ref, new_first_ref, new_second_ref,
):
    for b in range(BLOCKS):
        cols = slice(b * BLOCK, (b + 1) * BLOCK)
        gradient = own_ref[:, cols]
        if b == 0:
            gradient = gradient + from_left_ref[...]
        if b == BLOCKS - 1:
            gradient = gradient + from_right_ref[...]
        new_first = beta_one * first_ref[:, cols] + (1 - beta_one) * gradient
        new_second = beta_two * second_ref[:, cols] + (1 - beta_two) * gradient * gradient
        update = (
            new_first
            / (1 - beta_one**adam_step)
            / (jnp.sqrt(new_second / (1 - beta_two**adam_step)) + tiny)
        )
        gradient_ref[:, cols] = gradient
        new_params_ref[:, cols] = params_ref[:, cols] - rate * update
        new_first_ref[:, cols] = new_first
        new_second_ref[:, cols] = new_second


def adam(own, from_left, from_right, params, first, second):
    return pl.pallas_call(
        adam_kernel,
        out_shape=(jax.ShapeDtypeStruct((PARAMS, BLOCKS * BLOCK), f32),) * 4,
        in_specs=[whole()] * 6,
        out_specs=(whole(),) * 4,
        name="adam",
    )(own, from_left, from_right, params, first, second)


def on_device(
    params,
    first_moment,
    second_moment,
    piece_blocks,
    piece_live,
    piece_owner,
    piece_cell,
    target,
    background,
):
    features = jnp.asarray(exponent_features())
    moments = jnp.asarray(moment_features())
    blocks = piece_blocks[0]
    low, high = swap(params, (BLOCKS - 1) * BLOCK, params, 0, 0, "cut_blocks")
    pieces, *tables = render(blocks, piece_live, params, low, high, features)
    cotangent = exchange(pieces, piece_owner, piece_cell, target, background)
    own, edge_low, edge_high = pull(
        blocks, piece_live, cotangent, params, low, high, features, moments, tables
    )
    from_left, from_right = swap(edge_high, 0, edge_low, 0, 2, "cut_gradients")
    return adam(own, from_left, from_right, params, first_moment, second_moment)


def solution(mesh):
    in_specs = (
        P(None, ("region", "dom")),
        P(None, ("region", "dom")),
        P(None, ("region", "dom")),
        P(("region", "dom"), None, None),
        P(("region", "dom"), None),
        P(("region", "dom"), None),
        P(("region", "dom"), None),
        P(("region", "dom"), None, None, None),
        P(),
    )
    out_specs = (
        P(None, ("region", "dom")),
        P(None, ("region", "dom")),
        P(None, ("region", "dom")),
        P(None, ("region", "dom")),
    )
    return jax.shard_map(
        on_device, mesh=mesh, in_specs=in_specs, out_specs=out_specs, check_vma=False
    )
```

time: 519 us -> 89.2 us (0.17)
  waiting for transfers between devices: 236 us -> 0 us
  other arithmetic: 98 us -> 0 us
  Pallas kernels: 0 us -> 78.3 us
  blocking collectives: 63.9 us -> 0 us
  matrix products: 60.6 us -> 0 us
  starting transfers between devices: 17.5 us -> 0 us
  local copies, waits for them, and re-layouts: 26.6 us -> 9.61 us
  between operations: 14.6 us -> 0.75 us
    reduce_scatter x1 -> x0, waiting for transfers between devices: 216 us -> none  [on_device(): lax.psum_scatter(jnp.dot(onehot, grid_grads, precision=lax.Precision.HIGH...]
    pallas_call x0 -> x6, Pallas kernels: none -> 78.3 us  [the longest x1 28 us: exchange(): pl.pallas_call(exchange_kernel, out_shape=jax.ShapeDtypeStruct((2 * PIECE...]
    all_gather x2 -> x0, blocking collectives: 63.9 us -> none  [the longest x1 34.4 us: on_device(): lax.all_gather(piece_owner, 'dom', axis=0, tiled=True)]
    dot_general x26 -> x0, matrix products: 60.6 us -> none  [the longest x24 52.7 us: render_piece(): jnp.dot(colour, weight, precision=lax.Precision.HIGHEST)]
    another operation x26 -> x0, other arithmetic: 42.2 us -> none  [the longest x24 42.2 us: render_piece(): before = carry_log[None, :] + jnp.cumsum(log_keep, axis=0) - log_keep]
    reduce_sum x11 -> x0, other arithmetic: 37.3 us -> none  [the longest x4 28.9 us: render_piece(): conic_yy[:, None] * offset_y * offset_y]
    ppermute x4 -> x0, starting transfers between devices: 17.4 us -> none  [the longest x2 10.4 us: extended(): lax.ppermute(lax.slice_in_dim(block, block.shape[dim] - width, None, axis...]
    all_gather x1 -> x0, waiting for transfers between devices: 16.3 us -> none  [on_device(): lax.all_gather(outbound, 'dom', axis=0, tiled=True)]
  transfers between devices with their start and end apart: 6 -> 0, of which waited for: 3 -> 0; matrix products, arithmetic and copies ran while one was open for 1% -> 0% of each run, Pallas kernels for 0% -> 0%
where the time goes in v1:
time: 89.2 us; the launch traced here: 88.6 us
  Pallas kernels  78.3 us (88%)
  local copies, waits for them, and re-layouts  9.61 us (11%)
    pallas_call x1, Pallas kernels, exchange(): pl.pallas_call(exchange_kernel, out_shape=jax.ShapeDtypeStruct((2 * PIECE...  28 us
    pallas_call x1, Pallas kernels, pull(): pl.pallas_call(backward_kernel, out_shape=(shape((PARAMS, BLOCKS * BLOCK)...  20.1 us
    pallas_call x2, Pallas kernels, swap(): pl.pallas_call(body, out_shape=(jax.ShapeDtypeStruct((PARAMS, BLOCK), f32...  15 us
    pallas_call x1, Pallas kernels, render(): pl.pallas_call(forward_kernel, out_shape=(shape((PIECES, 4 * PIX), f32),...  12.9 us
    unnamed x29, local copies, waits for them, and re-layouts  8.79 us
    pallas_call x1, Pallas kernels, adam(): pl.pallas_call(adam_kernel, out_shape=(jax.ShapeDtypeStruct((PARAMS, BLOC...  2.32 us

profile of v1, /device:TPU:1, one launch (start us, length us, event | category | flops | bytes accessed | tf_op | source)
XLA Modules:
  0.0 88.6 jit_solution(13994916480196192049)
XLA Ops:
  0.6 0.0 copy-start.5
  0.6 0.0 copy-start.1
  0.7 0.8 copy.17.blocks_ref
  1.5 0.8 copy.16.target_ref
  2.2 5.4 %cut_blocks.1 = (f32[59,128]{1,0:T(8,128)}, f32[59,128]{1,0:T(8,128)}) custom-call(f32[59,1024]{1,0:T(8,128)} %params_ref.5, f32[59,1024]{1,0:T(8,128)} %params_ref.5), custom_call_target="tpu_custom_call" | custom-call | tf_op jit(solution)/shard_map/cut_blocks/pallas_call | solution.py:582
  7.7 0.0 copy-start
  7.7 0.9 %copy-done = f32[59,1024]{1,0:T(8,128)S(1)} copy-done((f32[59,1024]{1,0:T(8,128)S(1)}, f32[59,1024]{1,0:T(8,128)}, u32[]{:S(2)}) %copy-start) | copy-done | bytes 241688
  8.6 1.0 %copy-done.2 = bf16[32,32,256]{2,1,0:T(8,128)(2,1)S(1)} copy-done((bf16[32,32,256]{2,1,0:T(8,128)(2,1)S(1)}, bf16[32,32,256]{2,1,0:T(8,128)(2,1)}, u32[]{:S(2)}) %copy-start.2) | copy-done | bytes 524312
  9.7 0.8 copy-done.6
  10.4 0.8 copy-done.7
  11.2 0.7 copy-done.10
  11.8 12.9 %render_forward.1 = (f32[32,1024]{1,0:T(8,128)S(1)}, bf16[11,128,32]{2,1,0:T(8,128)(2,1)S(1)}, bf16[11,128,64]{2,1,0:T(8,128)(2,1)S(1)}, f32[32,2,8,256]{3,2,1,0:T(8,128)S(1)}, f32[32,2,3,8,256]{4,3,2,1,0:T(8,128)S(1)}) custom-call(s32[32,2]{1,0:T(8,128)S(1)} %copy.17.blocks_ref, s32[1,32]{1,0:T(1,128)S(1)} %copy-done.10, f32[59,1024]{1,0:T(8,128)S(1)} %copy-done, ...), custom_call_target="tpu_custom_call" | custom-call | tf_op jit(solution)/shard_map/render_forward/pallas_call | solution.py:362
  24.7 0.0 copy-start.11
  24.7 0.6 copy-done.11
  25.4 0.7 copy-done.12
  26.0 0.7 copy-done.13
  26.7 28.0 %tiles_to_owners.1.cotangent_ref = f32[512,128]{1,0:T(8,128)S(1)} custom-call(f32[32,1024]{1,0:T(8,128)S(1)} %get-tuple-element.18.pieces_ref, s32[1,32]{1,0:T(1,128)S(1)} %copy-done.11, s32[1,32]{1,0:T(1,128)S(1)} %copy-done.12, f32[1,8,3,256]{3,2,1,0:T(4,128)S(1)} %copy.16.target_ref, f32[3]{0:T(128)S(1)} %copy-done.13), custom_call_target="tpu_custom_call" | custom-call | tf_op jit(solution)/shard_map/tiles_to_owners/pallas_call | solution.py:779
  54.7 0.0 copy-done.5
  54.8 20.1 %render_backward.1 = (f32[59,1024]{1,0:T(8,128)S(1)}, f32[59,128]{1,0:T(8,128)S(1)}, f32[59,128]{1,0:T(8,128)S(1)}) custom-call(s32[32,2]{1,0:T(8,128)S(1)} %copy.17.blocks_ref, s32[1,32]{1,0:T(1,128)S(1)} %copy-done.10, f32[512,128]{1,0:T(8,128)S(1)} %tiles_to_owners.1.cotangent_ref, f32[59,1024]{1,0:T(8,128)S(1)} %copy-done.1, f32[59,128]{1,0:T(8,128)S(1)} %copy-done.6, ...), custom_call_target="tpu_custom_call" | custom-call | tf_op jit(solution)/shard_map/render_backward/pallas_call | solution.py:530
  74.8 0.7 copy-done.4
  75.5 0.6 copy-done.8
  76.1 0.6 copy-done.9
  76.8 9.5 %cut_gradients.1 = (f32[59,128]{1,0:T(8,128)}, f32[59,128]{1,0:T(8,128)}) custom-call(f32[59,128]{1,0:T(8,128)} %copy-done.9, f32[59,128]{1,0:T(8,128)} %copy-done.8), custom_call_target="tpu_custom_call" | custom-call | tf_op jit(solution)/shard_map/cut_gradients/pallas_call | solution.py:582
  86.3 2.3 %adam.1 = (f32[59,1024]{1,0:T(8,128)}, f32[59,1024]{1,0:T(8,128)}, f32[59,1024]{1,0:T(8,128)}, f32[59,1024]{1,0:T(8,128)}) custom-call(f32[59,1024]{1,0:T(8,128)} %copy-done.4, f32[59,128]{1,0:T(8,128)} %get-tuple-element.26.from_left_ref, f32[59,128]{1,0:T(8,128)} %get-tuple-element.27.from_right_ref, f32[59,1024]{1,0:T(8,128)} %params_ref.5, ...), custom_call_target="tpu_custom_call" | custom-call | tf_op jit(solution)/shard_map/adam/pallas_call | solution.py:818
  (12 shorter events, 0.0 us)
Async XLA Ops:
  0.6 54.1 %copy-start.5 = (bf16[32,16,256]{2,1,0:T(8,128)(2,1)S(1)}, bf16[32,16,256]{2,1,0:T(8,128)(2,1)}, u32[]{:S(2)}) copy-start(bf16[32,16,256]{2,1,0:T(8,128)(2,1)} %constant.5.clone.moments_ref) | copy-start | bytes 786436
  0.6 54.1 %copy-start.1 = (f32[59,1024]{1,0:T(8,128)S(1)}, f32[59,1024]{1,0:T(8,128)}, u32[]{:S(2)}) copy-start(f32[59,1024]{1,0:T(8,128)} %params_ref.5) | copy-start | bytes 724996
  7.7 1.0 %copy-start = (f32[59,1024]{1,0:T(8,128)S(1)}, f32[59,1024]{1,0:T(8,128)}, u32[]{:S(2)}) copy-start(f32[59,1024]{1,0:T(8,128)} %params_ref.5) | copy-start | bytes 724996
  8.6 1.0 %copy-start.2 = (bf16[32,32,256]{2,1,0:T(8,128)(2,1)S(1)}, bf16[32,32,256]{2,1,0:T(8,128)(2,1)}, u32[]{:S(2)}) copy-start(bf16[32,32,256]{2,1,0:T(8,128)(2,1)} %constant.4.clone.features_ref) | copy-start | bytes 1572868
  9.7 0.8 copy-start.6
  10.4 0.8 copy-start.7
  11.2 0.7 copy-start.10
  11.8 42.9 %copy-start.3 = (bf16[32,32,256]{2,1,0:T(8,128)(2,1)S(1)}, bf16[32,32,256]{2,1,0:T(8,128)(2,1)}, u32[]{:S(2)}) copy-start(bf16[32,32,256]{2,1,0:T(8,128)(2,1)} %constant.4.clone.features_ref) | copy-start | bytes 1572868
  24.7 0.7 copy-start.11
  25.4 0.7 copy-start.12
  26.0 0.7 copy-start.13
  74.8 0.7 copy-start.4
  75.5 0.6 copy-start.8
  76.1 0.6 copy-start.9

commit v2 on v1

v2 whole, which is shorter than its diff:
```python
import math

import jax
import jax.numpy as jnp
import ml_dtypes
import numpy as np
from jax import lax
from jax.experimental import pallas as pl
from jax.experimental.pallas import tpu as pltpu
from jax.sharding import PartitionSpec as P

PARAMS = 59
TSIDE = 16
WIN = 8
BLOCK = 128
BLOCKS = 8
MAXD = 8
PIECES = 32
PIX = 256
TILE_DEV = 8
CELLS = 64
POOL = 10
SLOTS = 2
SUB = 8
STEPS = BLOCK // SUB
TAB = POOL + 1
PLANES = 16
ROWS = 64
COLS = 96
UNROLL = 4
HALVES = 2
WIDE = PIX // HALVES
LOW = BLOCKS
HIGH = BLOCKS + 1
DEAD = POOL
ORIGIN_X = 64.0
ORIGIN_Y = 32.0

harmonic_zero = 0.28209479177387814
harmonic_one = 0.4886025119029199
harmonic_two = (
    1.0925484305920792,
    -1.0925484305920792,
    0.31539156525252005,
    -1.0925484305920792,
    0.5462742152960396,
)
harmonic_three = (
    -0.5900435899266435,
    2.890611442640554,
    -0.4570457994644658,
    0.3731763325901154,
    -0.4570457994644658,
    1.445305721320277,
    -0.5900435899266435,
)
beta_one = 0.9
beta_two = 0.999
rate = 0.001
adam_step = 100
tiny = 1e-08

f32 = jnp.float32
bf16 = jnp.bfloat16
MESH = pl.DeviceIdType.MESH
VMEM_LIMIT = 32 * 1024 * 1024


def pixel_monomials():
    bf = ml_dtypes.bfloat16
    tile = np.arange(PIECES)[:, None]
    pixel = np.arange(PIX)[None, :]
    x = (TSIDE * (tile % WIN) + pixel % TSIDE + 0.5 - ORIGIN_X).astype(np.float32)
    y = (TSIDE * (tile // WIN) + pixel // TSIDE + 0.5 - ORIGIN_Y).astype(np.float32)

    def two(value):
        head = value.astype(bf).astype(np.float32)
        return [head, value - head]

    return [np.ones_like(x), x, y] + two(x * x) + two(x * y) + two(y * y)


def exponent_features():
    rows = [row for row in pixel_monomials() for _ in range(3)]
    rows += [np.zeros_like(rows[0])] * (32 - len(rows))
    return np.stack(rows, axis=1).astype(ml_dtypes.bfloat16)


def moment_features():
    rows = pixel_monomials()
    rows += [np.zeros_like(rows[0])] * (16 - len(rows))
    return np.stack(rows, axis=1).astype(ml_dtypes.bfloat16)


def split(value, parts):
    out = []
    rest = value
    for part in range(parts):
        head = rest.astype(bf16)
        out.append(head)
        if part < parts - 1:
            rest = rest - head.astype(f32)
    return out


def exact_pick(onehot, value):
    picks = onehot.astype(bf16)
    total = None
    for part in reversed(split(value, 3)):
        term = jnp.dot(picks, part, preferred_element_type=f32)
        total = term if total is None else total + term
    return total


def iota(shape, dim):
    return lax.broadcasted_iota(jnp.int32, shape, dim)


def to_column(row):
    n = row.shape[1]
    spread = jnp.broadcast_to(row, (n, n))
    return jnp.sum(jnp.where(iota((n, n), 0) == iota((n, n), 1), spread, 0.0), axis=1, keepdims=True)


def to_row(column):
    n = column.shape[0]
    spread = jnp.broadcast_to(column, (n, n))
    return jnp.sum(jnp.where(iota((n, n), 0) == iota((n, n), 1), spread, 0.0), axis=0, keepdims=True)


def geometry(mean_x, mean_y, mean_z, log_a, log_b, log_c, quat_w, quat_x, quat_y, quat_z):
    screen_px = float(WIN * TSIDE)
    scales = (jnp.exp(log_a), jnp.exp(log_b), jnp.exp(log_c))
    norm = 1.0 / jnp.sqrt(quat_w * quat_w + quat_x * quat_x + quat_y * quat_y + quat_z * quat_z)
    quat_w, quat_x, quat_y, quat_z = quat_w * norm, quat_x * norm, quat_y * norm, quat_z * norm
    rotation = [
        [
            1 - 2 * (quat_y * quat_y + quat_z * quat_z),
            2 * (quat_x * quat_y - quat_w * quat_z),
            2 * (quat_x * quat_z + quat_w * quat_y),
        ],
        [
            2 * (quat_x * quat_y + quat_w * quat_z),
            1 - 2 * (quat_x * quat_x + quat_z * quat_z),
            2 * (quat_y * quat_z - quat_w * quat_x),
        ],
        [
            2 * (quat_x * quat_z - quat_w * quat_y),
            2 * (quat_y * quat_z + quat_w * quat_x),
            1 - 2 * (quat_x * quat_x + quat_y * quat_y),
        ],
    ]
    focal_px = 0.3125 * screen_px
    inv_z = 1.0 / mean_z
    ratio_x, ratio_y = mean_x * inv_z, mean_y * inv_z
    focal_z = focal_px * inv_z
    rows = []
    for ratio, axis in ((ratio_x, 0), (ratio_y, 1)):
        rows.append(
            [
                focal_z * (rotation[axis][col] - ratio * rotation[2][col]) * scales[col]
                for col in range(3)
            ]
        )
    sigma_xx = rows[0][0] * rows[0][0] + rows[0][1] * rows[0][1] + rows[0][2] * rows[0][2] + 0.3
    sigma_xy = rows[0][0] * rows[1][0] + rows[0][1] * rows[1][1] + rows[0][2] * rows[1][2]
    sigma_yy = rows[1][0] * rows[1][0] + rows[1][1] * rows[1][1] + rows[1][2] * rows[1][2] + 0.3
    inv_det = 1.0 / (sigma_xx * sigma_yy - sigma_xy * sigma_xy)
    return (
        focal_px * ratio_x + (0.5 * screen_px - ORIGIN_X),
        focal_px * ratio_y + (0.5 * screen_px - ORIGIN_Y),
        sigma_yy * inv_det,
        -sigma_xy * inv_det,
        sigma_xx * inv_det,
    )


def harmonics(mean_x, mean_y, mean_z):
    inv_length = 1.0 / jnp.sqrt(mean_x * mean_x + mean_y * mean_y + mean_z * mean_z)
    dir_x, dir_y, dir_z = mean_x * inv_length, mean_y * inv_length, mean_z * inv_length
    sq_x, sq_y, sq_z = dir_x * dir_x, dir_y * dir_y, dir_z * dir_z
    return (
        -harmonic_one * dir_y,
        harmonic_one * dir_z,
        -harmonic_one * dir_x,
        harmonic_two[0] * dir_x * dir_y,
        harmonic_two[1] * dir_y * dir_z,
        harmonic_two[2] * (2 * sq_z - sq_x - sq_y),
        harmonic_two[3] * dir_x * dir_z,
        harmonic_two[4] * (sq_x - sq_y),
        harmonic_three[0] * dir_y * (3 * sq_x - sq_y),
        harmonic_three[1] * dir_x * dir_y * dir_z,
        harmonic_three[2] * dir_y * (4 * sq_z - sq_x - sq_y),
        harmonic_three[3] * dir_z * (2 * sq_z - 3 * sq_x - 3 * sq_y),
        harmonic_three[4] * dir_x * (4 * sq_z - sq_x - sq_y),
        harmonic_three[5] * dir_z * (sq_x - sq_y),
        harmonic_three[6] * dir_x * (sq_x - 3 * sq_y),
    )


def plane(ref, half, row):
    return ref[pl.ds(half * SUB * ROWS + row, SUB, stride=ROWS), :]


def put_plane(ref, half, row, value):
    ref[pl.ds(half * SUB * ROWS + row, SUB, stride=ROWS), :] = value


def raw_colour(pool, half, basis, colour):
    total = harmonic_zero * plane(pool, half, 11 + 16 * colour) + 0.5
    for k in range(1, 16):
        total = total + plane(pool, half, 11 + 16 * colour + k) * basis[k - 1]
    return total


def own_block(number):
    return jnp.where(number == 0, LOW, jnp.where(number == POOL - 1, HIGH, number - 1))


def roll_rows(value, shift):
    return pltpu.roll(value, shift % SUB, axis=0)


def tabulate(half, count, pool, stage, turned, table, spread):
    region = lax.axis_index("region")
    regions = lax.axis_size("region")
    means = [plane(pool, half, r) for r in range(3)]
    centre_u, centre_v, conic_xx, conic_xy, conic_yy = geometry(
        *means, *[plane(pool, half, r) for r in range(3, 10)]
    )
    opacity = 1.0 / (1.0 + jnp.exp(-plane(pool, half, 10)))
    log2_e = 1.0 / math.log(2.0)
    slope_x = conic_xx * centre_u + conic_xy * centre_v
    slope_y = conic_xy * centre_u + conic_yy * centre_v
    constant = jnp.log(opacity) - 0.5 * (centre_u * slope_x + centre_v * slope_y)
    constant = log2_e * constant
    if half:
        row = iota((SUB, BLOCK), 0)
        absent = ((row == LOW - SUB) & (region == 0)) | ((row == HIGH - SUB) & (region == regions - 1))
        constant = jnp.where(absent, -1e30, constant)
    terms = [
        constant,
        log2_e * slope_x,
        log2_e * slope_y,
        (-0.5 * log2_e) * conic_xx,
        (-log2_e) * conic_xy,
        (-0.5 * log2_e) * conic_yy,
    ]
    stage[...] = jnp.zeros_like(stage)

    def put(row, value):
        stage[pl.ds(row, SUB, stride=COLS), :] = value

    row = 0
    for term, copies in zip(terms, (1, 1, 1, 2, 2, 2)):
        parts = [part.astype(f32) for part in split(term, 3)]
        for _ in range(copies):
            for part in parts:
                put(row, part)
                row += 1
    basis = harmonics(*means)
    for c in range(3):
        tone = jnp.maximum(raw_colour(pool, half, basis, c), 0.0)
        parts = [part.astype(f32) for part in split(tone, 3)]
        for group, part in enumerate((0, 0, 0, 1, 1, 2)):
            put(32 + group * SUB + c, parts[part])
        put(80 + c, tone)

    def turn(b, carry):
        turned[:, :COLS] = stage[pl.ds(pl.multiple_of(b * COLS, COLS), COLS), :].T
        ordered = jnp.concatenate(
            [turned[pl.ds(t, SUB, stride=STEPS), :] for t in range(STEPS)], axis=0
        )
        table[half * SUB + b] = ordered[:, :COLS].astype(bf16)
        for c in range(3):
            spread[half * SUB + b, c] = jnp.broadcast_to(ordered[:, 80 + c : 81 + c], (BLOCK, BLOCK))
        return carry

    lax.fori_loop(0, count, turn, 0, unroll=2)


def exponents(table, features, block):
    return jnp.dot(table[block, :, :32], features, preferred_element_type=f32)


def two_blocks(p, blocks, live):
    first = own_block(blocks[0, p])
    second = jnp.where(live[0, p] > 1, own_block(blocks[1, p]), DEAD)
    return first, second


def forward_half(h, blocks, live, features_ref, table, spread, prefix_ref, segment_ref, pieces):
    sub = iota((SUB, WIDE), 0)

    def piece(p, carry):
        features = features_ref[p, :, h * WIDE : (h + 1) * WIDE]
        before = None
        colours = [None] * 3
        for j, block in enumerate(two_blocks(p, blocks, live)):
            exponent = exponents(table, features, block)
            transmit = jnp.ones((SUB, WIDE), f32)
            sums = [jnp.zeros((SUB, WIDE), f32) for _ in range(3)]
            for t in range(STEPS):
                rows = slice(t * SUB, (t + 1) * SUB)
                weight = jnp.exp2(exponent[rows]) * transmit
                transmit = transmit - weight
                for c in range(3):
                    tone = spread[block, c, rows, :]
                    tone = tone if WIDE == BLOCK else jnp.concatenate([tone, tone], axis=1)
                    sums[c] = sums[c] + tone * weight
            run = transmit
            for shift in (1, 2, 4):
                run = run * jnp.where(sub >= shift, roll_rows(run, shift), 1.0)
            prefix = jnp.where(sub >= 1, roll_rows(run, 1), 1.0)
            total = run[SUB - 1 :, :]
            if before is not None:
                prefix = prefix * before
                total = total * before
            before = total
            prefix_ref[h, p, j] = prefix
            for c in range(3):
                piece_sum = prefix * sums[c]
                segment_ref[h, p, j, c] = piece_sum
                colours[c] = piece_sum if j == 0 else colours[c] + piece_sum
        rows = [jnp.sum(colours[c], axis=0, keepdims=True) for c in range(3)] + [1.0 - before]
        for c in range(4):
            for k in range(WIDE // BLOCK):
                place = (c * (WIDE // BLOCK) + k) * PIECES + p
                pieces[pl.ds(place, 1), :] = rows[c][:, k * BLOCK : (k + 1) * BLOCK]
        return carry

    lax.fori_loop(0, PIECES, piece, 0, unroll=UNROLL)


def backward_half(
    h, blocks, live, features_ref, moments_ref, table, prefix_ref, segment_ref, cotangent, moved
):
    sub = iota((SUB, WIDE), 0)
    nothing = jnp.zeros((16, WIDE), bf16)
    none = jnp.zeros((16, WIDE), f32)
    lanes = slice(h * WIDE, (h + 1) * WIDE)

    def piece(p, carry):
        features = features_ref[p, :, lanes]
        monomials = moments_ref[p, :, lanes]
        cot = jnp.concatenate(
            [
                cotangent[pl.ds(pl.multiple_of((k * PIECES + p) * SUB, SUB), SUB), :]
                for k in range(WIDE // BLOCK)
            ],
            axis=1,
        )
        heads = [part.astype(f32) for part in split(cot, 3)]
        tones = [none, none] + [heads[part] for part in (0, 1, 2, 0, 1, 0)] + [none]
        tones = jnp.concatenate(tones, axis=0).astype(bf16)
        colour_rows = jnp.concatenate([heads[0], heads[1]], axis=0).astype(bf16)
        for_gradient = jnp.concatenate([monomials, nothing], axis=0)
        for_weight = jnp.concatenate([nothing, colour_rows], axis=0)
        state = []
        for j, block in enumerate(two_blocks(p, blocks, live)):
            exponent = exponents(table, features, block)
            tone = jnp.dot(table[block], tones, preferred_element_type=f32)
            transmit = prefix_ref[h, p, j]
            alphas, weights = [], []
            for t in range(STEPS):
                alpha = jnp.exp2(exponent[t * SUB : (t + 1) * SUB])
                weight = alpha * transmit
                transmit = transmit - weight
                alphas.append(alpha)
                weights.append(weight)
            seen = segment_ref[h, p, j, 0] * cot[0:1]
            for c in (1, 2):
                seen = seen + segment_ref[h, p, j, c] * cot[c : c + 1]
            run = seen
            for shift in (1, 2, 4):
                run = run + jnp.where(sub < SUB - shift, roll_rows(run, -shift), 0.0)
            state.append((tone, transmit, alphas, weights, run))
        behind = state[1][1][SUB - 1 :, :] * cot[3:4]
        parts = [None, None]
        for j in (1, 0):
            tone, transmit, alphas, weights, run = state[j]
            after = jnp.where(sub < SUB - 1, roll_rows(run, -1), 0.0) + behind
            behind = behind + run[0:1]
            ahead = after / transmit
            gradients = [None] * STEPS
            for t in reversed(range(STEPS)):
                gap = tone[t * SUB : (t + 1) * SUB] - ahead
                gradients[t] = weights[t] * gap
                ahead = ahead + alphas[t] * gap
            parts[j] = split(jnp.concatenate(gradients, axis=0), 2)
            parts[j] += split(jnp.concatenate(weights, axis=0), 2)
        total = None
        for k in range(4):
            term = lax.dot_general(
                (for_gradient, for_weight)[k // 2],
                jnp.concatenate([parts[0][k], parts[1][k]], axis=0),
                (((1,), (1,)), ((), ())),
                preferred_element_type=f32,
            )
            total = term if total is None else total + term
        for j in range(2):
            rows = pl.ds(pl.multiple_of((j * PIECES + p) * 32, 32), 32)
            part = total[:, j * BLOCK : (j + 1) * BLOCK]
            moved[rows, :] = part if h == 0 else moved[rows, :] + part
        return carry

    lax.fori_loop(0, PIECES, piece, 0, unroll=UNROLL)


def gather_moments(first_row, second_row, moved, summed):
    numbers = iota((2 * SUB, PIECES), 0).astype(f32)
    lane = iota((BLOCK, BLOCK), 0)
    unshuffle = (lane % SUB) * STEPS + lane // SUB == iota((BLOCK, BLOCK), 1)
    unshuffle = jnp.where(unshuffle, 1.0, 0.0).astype(bf16)
    for group in range(3):
        features = range(group * SUB, group * SUB + SUB)
        features = [f for f in features if f < 9] + [16 + f - 9 for f in features if 9 <= f < 12]
        features += [24 + f - 12 for f in range(group * SUB, group * SUB + SUB) if 12 <= f < 15]
        if not features:
            continue
        total = None
        for j, row in enumerate((first_row, second_row)):
            pick = jnp.where(jnp.broadcast_to(row, (2 * SUB, PIECES)) == numbers, 1.0, 0.0)
            values = [
                moved[pl.ds(j * PIECES * 32 + f, PIECES, stride=32), :] for f in features
            ]
            term = exact_pick(pick, jnp.concatenate(values, axis=1))
            total = term if total is None else total + term
        stacked = jnp.concatenate(
            [total[:, k * BLOCK : (k + 1) * BLOCK] for k in range(len(features))], axis=0
        )
        ordered = None
        for part in reversed(split(stacked, 3)):
            term = jnp.dot(part, unshuffle, preferred_element_type=f32)
            ordered = term if ordered is None else ordered + term
        for k, f in enumerate(features):
            summed[f] = ordered[k * 2 * SUB : (k + 1) * 2 * SUB]


def pull_splat(half, pool, summed, grads_ref):
    means = [plane(pool, half, r) for r in range(3)]
    (centre_u, centre_v, conic_xx, conic_xy, conic_yy), geometry_pull = jax.vjp(
        geometry, *means, *[plane(pool, half, r) for r in range(3, 10)]
    )
    basis, harmonics_pull = jax.vjp(harmonics, *means)
    opacity = 1.0 / (1.0 + jnp.exp(-plane(pool, half, 10)))
    sums = [summed[f, half * SUB : (half + 1) * SUB] for f in range(9)]
    total, sum_x, sum_y = sums[:3]
    sum_xx, sum_xy, sum_yy = sums[3] + sums[4], sums[5] + sums[6], sums[7] + sums[8]
    off_x = sum_x - centre_u * total
    off_y = sum_y - centre_v * total
    grad_xx = -0.5 * (sum_xx - centre_u * (sum_x + off_x))
    grad_xy = -(sum_xy - centre_u * sum_y - centre_v * off_x)
    grad_yy = -0.5 * (sum_yy - centre_v * (sum_y + off_y))
    grad_u = conic_xx * off_x + conic_xy * off_y
    grad_v = conic_xy * off_x + conic_yy * off_y
    grads = geometry_pull((grad_u, grad_v, grad_xx, grad_xy, grad_yy))
    tone_grads = []
    for c in range(3):
        grad = summed[16 + c, half * SUB : (half + 1) * SUB] + summed[24 + c, half * SUB : (half + 1) * SUB]
        raw = raw_colour(pool, half, basis, c)
        tone_grads.append(jnp.where(raw > 0, grad, jnp.where(raw == 0, 0.5 * grad, 0.0)))
    basis_grads = []
    for k in range(1, 16):
        basis_grads.append(
            sum(tone_grads[c] * plane(pool, half, 11 + 16 * c + k) for c in range(3))
        )
    mean_grads = harmonics_pull(tuple(basis_grads))
    for r in range(10):
        put_plane(grads_ref, half, r, grads[r] + mean_grads[r] if r < 3 else grads[r])
    put_plane(grads_ref, half, 10, total * (1.0 - opacity))
    for c in range(3):
        put_plane(grads_ref, half, 11 + 16 * c, tone_grads[c] * harmonic_zero)
        for k in range(1, 16):
            put_plane(grads_ref, half, 11 + 16 * c + k, tone_grads[c] * basis[k - 1])


PARTS = 4 * WIDE // BLOCK
MESSAGE = SLOTS * PARTS


def put_slots(ref, values):
    for k in range(SLOTS):
        for r in range(PARTS):
            ref[pl.ds(k * PARTS + r, 32, stride=MESSAGE), :] = values[
                k * 32 : (k + 1) * 32, r * BLOCK : (r + 1) * BLOCK
            ]


def get_slots(ref):
    return jnp.concatenate(
        [
            jnp.concatenate(
                [ref[pl.ds(k * PARTS + r, 32, stride=MESSAGE), :] for r in range(PARTS)], axis=1
            )
            for k in range(SLOTS)
        ],
        axis=0,
    )


def route(owner_row, cell_row, me):
    owner_col = to_column(owner_row)
    far_row = owner_row - me.astype(f32)
    far_row = jnp.where(far_row < 0, far_row + float(PIECES), far_row)
    far_col = to_column(far_row)
    square = (PIECES, PIECES)
    same = jnp.broadcast_to(owner_row, square) == jnp.broadcast_to(owner_col, square)
    first, second = iota(square, 0), iota(square, 1)
    rank_row = jnp.sum(jnp.where(same & (first < second), 1.0, 0.0), axis=0, keepdims=True)
    rank_col = jnp.sum(jnp.where(same & (second < first), 1.0, 0.0), axis=1, keepdims=True)
    slots = SLOTS * 32
    pack = jnp.broadcast_to(rank_row * 32.0 + far_row, (slots, PIECES)) == iota((slots, PIECES), 0).astype(f32)
    pack = jnp.where(pack, 1.0, 0.0)
    unpack = jnp.broadcast_to(rank_col * 32.0 + far_col, (PIECES, slots)) == iota((PIECES, slots), 1).astype(f32)
    unpack = jnp.where(unpack, 1.0, 0.0)
    label_col = jnp.sum(pack * (cell_row + 1.0), axis=1, keepdims=True) - 1.0
    lane = iota((32, BLOCK), 1)
    label_rows = jnp.where(lane == 0, label_col[:32], jnp.where(lane == 1, label_col[32:], -1.0))
    return pack, unpack, label_rows


def composite(h, grid, target, background):
    def at(depth, channel):
        return grid[depth * SUB : (depth + 1) * SUB, channel * WIDE : (channel + 1) * WIDE]

    in_front = jnp.ones((TILE_DEV, WIDE), f32)
    seen = [jnp.zeros((TILE_DEV, WIDE), f32) for _ in range(3)]
    fronts = []
    for depth in range(MAXD):
        fronts.append(in_front)
        seen = [seen[c] + in_front * at(depth, c) for c in range(3)]
        in_front = in_front * (1.0 - at(depth, 3))
    residual = [
        seen[c] + in_front * background[c] - target[c, :, h * WIDE : (h + 1) * WIDE] for c in range(3)
    ]
    behind = [jnp.full((TILE_DEV, WIDE), background[c], f32) for c in range(3)]
    rows = [None] * MAXD
    for depth in reversed(range(MAXD)):
        through = 1.0 - at(depth, 3)
        by_trans = residual[0] * behind[0] + residual[1] * behind[1] + residual[2] * behind[2]
        rows[depth] = jnp.concatenate(
            [fronts[depth] * residual[c] for c in range(3)] + [fronts[depth] * by_trans], axis=1
        )
        behind = [at(depth, c) + through * behind[c] for c in range(3)]
    return jnp.concatenate(rows, axis=0)


def step_kernel(
    params_hbm,
    blocks_hbm,
    live_hbm,
    owner_hbm,
    cell_hbm,
    target_hbm,
    background_hbm,
    features_hbm,
    moments_hbm,
    grads_ref,
    from_left,
    from_right,
    blocks,
    live,
    background,
    block_rows,
    owner,
    cell,
    target,
    features,
    moments,
    pool,
    stage,
    turned,
    table,
    spread,
    prefix,
    segment,
    pieces,
    sent,
    got,
    replies,
    answers,
    labels,
    got_labels,
    cotangent,
    moved,
    summed,
    local_sem,
    halo_send,
    halo_recv,
    edge_send,
    edge_recv,
    label_send,
    label_recv,
    send_sem,
    recv_sem,
    reply_send,
    reply_recv,
):
    regions, region = lax.axis_size("region"), lax.axis_index("region")
    count, me = lax.axis_size("dom"), lax.axis_index("dom")
    upper, lower = lax.rem(region + 1, regions), lax.rem(region + regions - 1, regions)

    def block_rows_of(ref, b):
        return ref.at[pl.ds(b * ROWS, PARAMS)]

    fetches = []

    def fetch(src, dst):
        copy = pltpu.make_async_copy(src, dst, local_sem.at[len(fetches)])
        copy.start()
        fetches.append(copy)
        return copy

    routing = [fetch(owner_hbm, owner), fetch(cell_hbm, cell)]
    own = [
        fetch(params_hbm.at[:, pl.ds(b * BLOCK, BLOCK)], block_rows_of(pool, b)) for b in range(BLOCKS)
    ]
    scalars = [fetch(blocks_hbm, blocks), fetch(live_hbm, live), fetch(features_hbm, features)]
    later = [
        fetch(blocks_hbm, block_rows),
        fetch(target_hbm, target),
        fetch(background_hbm, background),
        fetch(moments_hbm, moments),
    ]

    barrier = pltpu.get_barrier_semaphore()

    def signal(**where):
        pl.semaphore_signal(barrier, inc=1, device_id=where, device_id_type=MESH)

    def greet(d, carry):
        signal(dom=lax.rem(me + d, count))
        return carry

    signal(region=upper)
    signal(region=lower)
    lax.fori_loop(1, count, greet, 0)

    for copy in routing:
        copy.wait()
    pack, unpack, label_rows = route(owner[...].astype(f32), cell[...].astype(f32), me)
    for d in range(32):
        labels[d] = label_rows[d : d + 1]
    pl.semaphore_wait(barrier, count + 1)

    def remote(src, dst, send, recv, **where):
        return pltpu.make_async_remote_copy(
            src_ref=src, dst_ref=dst, send_sem=send, recv_sem=recv, device_id=where, device_id_type=MESH
        )

    def label(d):
        where = lax.rem(me + d, count)
        return remote(labels.at[d], got_labels.at[d], label_send.at[d], label_recv.at[d], dom=where)

    def message(d):
        return pl.ds(pl.multiple_of(d * MESSAGE, MESSAGE), MESSAGE)

    def payload(h, d):
        where = lax.rem(me + d, count)
        rows = message(d)
        return remote(sent.at[h, rows], got.at[h, rows], send_sem.at[h, d], recv_sem.at[h, d], dom=where)

    def reply(h, d):
        where = lax.rem(me + count - d, count)
        rows = message(d)
        return remote(
            replies.at[h, rows], answers.at[h, rows], reply_send.at[h, d], reply_recv.at[h, d], dom=where
        )

    def for_all(act):
        def one(d, carry):
            act(d)
            return carry

        lax.fori_loop(1, count, one, 0)

    halo = [
        remote(
            params_hbm.at[:, pl.ds((BLOCKS - 1) * BLOCK, BLOCK)],
            block_rows_of(pool, LOW),
            halo_send.at[0],
            halo_recv.at[0],
            region=upper,
        ),
        remote(
            params_hbm.at[:, pl.ds(0, BLOCK)],
            block_rows_of(pool, HIGH),
            halo_send.at[1],
            halo_recv.at[1],
            region=lower,
        ),
    ]
    for copy in halo:
        copy.start()
    for_all(lambda d: label(d).start())
    got_labels[0] = labels[0]

    for copy in own:
        copy.wait()
    for b in range(POOL, 2 * SUB):
        pool[b * ROWS : b * ROWS + PARAMS, :] = pool[0:PARAMS, :]
    tabulate(0, SUB, pool, stage, turned, table, spread)
    for copy in halo:
        copy.wait_recv()
    tabulate(1, POOL - SUB, pool, stage, turned, table, spread)
    lane = iota((BLOCK, COLS), 1)
    table[DEAD] = jnp.where(lane == 0, -1e30, 0.0).astype(bf16)
    spread[DEAD] = jnp.zeros((3, BLOCK, BLOCK), f32)

    for copy in scalars:
        copy.wait()
    for h in range(HALVES):
        forward_half(h, blocks, live, features, table, spread, prefix, segment, pieces)
        rendered = [pieces[r * PIECES : (r + 1) * PIECES, :] for r in range(PARTS)]
        rendered = jnp.concatenate(rendered, axis=1)
        put_slots(sent.at[h], exact_pick(pack, rendered))
        for_all(lambda d: payload(h, d).start())
        got[h, :MESSAGE] = sent[h, :MESSAGE]

    for copy in later:
        copy.wait()
    for_all(lambda d: label(d).wait())
    arrived = jnp.concatenate([got_labels[d] for d in range(32)], axis=0)
    arrived_col = jnp.concatenate([arrived[:, 0:1], arrived[:, 1:2]], axis=0)
    arrived_row = to_row(arrived_col)
    slots = SLOTS * 32

    def cell_of(place):
        return ((place % TILE_DEV) * MAXD + place // TILE_DEV).astype(f32)

    gather = jnp.broadcast_to(arrived_row, (CELLS, slots)) == cell_of(iota((CELLS, slots), 0))
    gather = jnp.where(gather, 1.0, 0.0)
    scatter = jnp.broadcast_to(arrived_col, (slots, CELLS)) == cell_of(iota((slots, CELLS), 1))
    scatter = jnp.where(scatter, 1.0, 0.0)
    colours = [background[c] for c in range(3)]
    for h in range(HALVES):
        for_all(lambda d: payload(h, d).wait())
        grid = exact_pick(gather, get_slots(got.at[h]))
        put_slots(replies.at[h], exact_pick(scatter, composite(h, grid, target, colours)))
        for_all(lambda d: reply(h, d).start())
        answers[h, :MESSAGE] = replies[h, :MESSAGE]

    for h in range(HALVES):
        for_all(lambda d: reply(h, d).wait())
        back = exact_pick(unpack, get_slots(answers.at[h]))
        for k in range(WIDE // BLOCK):
            for c in range(SUB):
                lanes = slice(c * WIDE + k * BLOCK, c * WIDE + (k + 1) * BLOCK)
                rows = back[:, lanes] if c < 4 else jnp.zeros((PIECES, BLOCK), f32)
                cotangent[pl.ds(k * PIECES * SUB + c, PIECES, stride=SUB), :] = rows
        backward_half(
            h, blocks, live, features, moments, table, prefix, segment, cotangent, moved
        )

    rows = own_block(block_rows[...]).astype(f32)
    gather_moments(rows[0:1], rows[1:2], moved, summed)
    pull_splat(1, pool, summed, grads_ref)
    edges = [
        remote(block_rows_of(grads_ref, HIGH), from_left, edge_send.at[0], edge_recv.at[0], region=upper),
        remote(block_rows_of(grads_ref, LOW), from_right, edge_send.at[1], edge_recv.at[1], region=lower),
    ]
    for copy in edges:
        copy.start()
    pull_splat(0, pool, summed, grads_ref)
    for copy in halo:
        copy.wait_send()
    for copy in edges:
        copy.wait()


def whole(memory=pltpu.VMEM):
    return pl.BlockSpec(memory_space=memory)


def step(*operands):
    shape = jax.ShapeDtypeStruct
    vmem, smem, dma = pltpu.VMEM, pltpu.SMEM, pltpu.SemaphoreType.DMA
    slots = vmem((HALVES, 32 * MESSAGE, BLOCK), f32)
    label = vmem((32, 1, BLOCK), f32)
    return pl.pallas_call(
        step_kernel,
        out_shape=(
            shape((2 * SUB * ROWS, BLOCK), f32),
            shape((PARAMS, BLOCK), f32),
            shape((PARAMS, BLOCK), f32),
        ),
        in_specs=[whole(pl.ANY)] * 9,
        out_specs=(whole(),) * 3,
        scratch_shapes=[
            smem((2, PIECES), jnp.int32),
            smem((1, PIECES), jnp.int32),
            smem((3,), f32),
            vmem((2, PIECES), jnp.int32),
            vmem((1, PIECES), jnp.int32),
            vmem((1, PIECES), jnp.int32),
            vmem((3, TILE_DEV, PIX), f32),
            vmem((PIECES, 32, PIX), bf16),
            vmem((PIECES, 16, PIX), bf16),
            vmem((2 * SUB * ROWS, BLOCK), f32),
            vmem((SUB * COLS, BLOCK), f32),
            vmem((BLOCK, BLOCK), f32),
            vmem((TAB, BLOCK, COLS), bf16),
            vmem((TAB, 3, BLOCK, BLOCK), f32),
            vmem((HALVES, PIECES, 2, SUB, WIDE), f32),
            vmem((HALVES, PIECES, 2, 3, SUB, WIDE), f32),
            vmem((4 * WIDE // BLOCK * PIECES, BLOCK), f32),
            slots,
            slots,
            slots,
            slots,
            label,
            label,
            vmem((WIDE // BLOCK * PIECES * SUB, BLOCK), f32),
            vmem((2 * PIECES * 32, BLOCK), f32),
            vmem((32, 2 * SUB, BLOCK), f32),
            dma((17,)),
            dma((2,)),
            dma((2,)),
            dma((2,)),
            dma((2,)),
            dma((32,)),
            dma((32,)),
            dma((HALVES, 32)),
            dma((HALVES, 32)),
            dma((HALVES, 32)),
            dma((HALVES, 32)),
        ],
        compiler_params=pltpu.CompilerParams(
            collective_id=0, has_side_effects=True, vmem_limit_bytes=VMEM_LIMIT
        ),
        name="render_step",
    )(*operands)


def adam_kernel(
    grads_ref, from_left_ref, from_right_ref, params_ref, first_ref, second_ref,
    gradient_ref, new_params_ref, new_first_ref, new_second_ref,
):
    for b in range(BLOCKS):
        cols = slice(b * BLOCK, (b + 1) * BLOCK)
        gradient = grads_ref[b * ROWS : b * ROWS + PARAMS, :]
        if b == 0:
            gradient = gradient + from_left_ref[...]
        if b == BLOCKS - 1:
            gradient = gradient + from_right_ref[...]
        new_first = beta_one * first_ref[:, cols] + (1 - beta_one) * gradient
        new_second = beta_two * second_ref[:, cols] + (1 - beta_two) * gradient * gradient
        update = (
            new_first
            / (1 - beta_one**adam_step)
            / (jnp.sqrt(new_second / (1 - beta_two**adam_step)) + tiny)
        )
        gradient_ref[:, cols] = gradient
        new_params_ref[:, cols] = params_ref[:, cols] - rate * update
        new_first_ref[:, cols] = new_first
        new_second_ref[:, cols] = new_second


def adam(*operands):
    return pl.pallas_call(
        adam_kernel,
        out_shape=(jax.ShapeDtypeStruct((PARAMS, BLOCKS * BLOCK), f32),) * 4,
        in_specs=[whole()] * 6,
        out_specs=(whole(),) * 4,
        compiler_params=pltpu.CompilerParams(vmem_limit_bytes=8 * 1024 * 1024),
        name="adam",
    )(*operands)


def on_device(
    params,
    first_moment,
    second_moment,
    piece_blocks,
    piece_live,
    piece_owner,
    piece_cell,
    target,
    background,
):
    grads, from_left, from_right = step(
        params,
        piece_blocks[0].T,
        piece_live,
        piece_owner,
        piece_cell,
        jnp.transpose(target[0], (1, 0, 2)),
        background,
        jnp.asarray(exponent_features()),
        jnp.asarray(moment_features()),
    )
    return adam(grads, from_left, from_right, params, first_moment, second_moment)


def solution(mesh):
    in_specs = (
        P(None, ("region", "dom")),
        P(None, ("region", "dom")),
        P(None, ("region", "dom")),
        P(("region", "dom"), None, None),
        P(("region", "dom"), None),
        P(("region", "dom"), None),
        P(("region", "dom"), None),
        P(("region", "dom"), None, None, None),
        P(),
    )
    out_specs = (
        P(None, ("region", "dom")),
        P(None, ("region", "dom")),
        P(None, ("region", "dom")),
        P(None, ("region", "dom")),
    )
    return jax.shard_map(
        on_device, mesh=mesh, in_specs=in_specs, out_specs=out_specs, check_vma=False
    )
```

time: 89.2 us -> 62.4 us (0.70)
  Pallas kernels: 78.3 us -> 57.1 us
  local copies, waits for them, and re-layouts: 9.61 us -> 4.37 us
    pallas_call x5 -> x1, Pallas kernels: 75.9 us -> 56 us  [step(): pl.pallas_call(step_kernel, out_shape=(shape((2 * SUB * ROWS, BLOCK), f32...]
    unnamed x29 -> x22, local copies, waits for them, and re-layouts: 8.79 us -> 4.37 us
    pallas_call x1, Pallas kernels: 2.32 us -> 1.11 us  [adam(): pl.pallas_call(adam_kernel, out_shape=(jax.ShapeDtypeStruct((PARAMS, BLOC...]
where the time goes in v2:
time: 62.4 us; the launch traced here: 62.2 us
  Pallas kernels  57.1 us (92%)
  local copies, waits for them, and re-layouts  4.37 us (7%)
  between operations  0.71 us (1%)
    pallas_call x1, Pallas kernels, step(): pl.pallas_call(step_kernel, out_shape=(shape((2 * SUB * ROWS, BLOCK), f32...  56 us
    unnamed x22, local copies, waits for them, and re-layouts  4.37 us

profile of v2, /device:TPU:1, one launch (start us, length us, event | category | flops | bytes accessed | tf_op | source)
XLA Modules:
  0.0 62.2 jit_solution(3504825668795786867)
XLA Ops:
  0.6 0.0 copy-start.8
  0.6 0.0 copy-start.9
  0.7 0.0 copy-start.10
  0.7 0.0 copy-start.6
  0.7 0.0 copy-start.7
  0.7 0.6 copy-done.8
  1.3 0.0 copy-done.9
  1.3 0.0 copy-done.10
  1.3 0.0 copy-done.6
  1.4 0.0 copy-done.7
  1.4 0.0 copy-start
  1.4 0.9 %copy-done = f32[59,1024]{1,0:T(8,128)S(1)} copy-done((f32[59,1024]{1,0:T(8,128)S(1)}, f32[59,1024]{1,0:T(8,128)}, u32[]{:S(2)}) %copy-start) | copy-done | bytes 241688
  2.3 0.0 copy-start.1
  2.3 1.0 %copy-done.1 = bf16[32,32,256]{2,1,0:T(8,128)(2,1)S(1)} copy-done((bf16[32,32,256]{2,1,0:T(8,128)(2,1)S(1)}, bf16[32,32,256]{2,1,0:T(8,128)(2,1)}, u32[]{:S(2)}) %copy-start.1) | copy-done | bytes 524312
  3.4 0.0 copy-start.2
  3.4 0.9 %copy-done.2 = bf16[32,16,256]{2,1,0:T(8,128)(2,1)S(1)} copy-done((bf16[32,16,256]{2,1,0:T(8,128)(2,1)S(1)}, bf16[32,16,256]{2,1,0:T(8,128)(2,1)}, u32[]{:S(2)}) %copy-start.2) | copy-done | bytes 262168
  4.3 0.0 copy-start.5
  4.3 0.7 %copy-done.5 = f32[1,8,3,256]{3,1,2,0:T(8,128)S(1)} copy-done((f32[1,8,3,256]{3,1,2,0:T(8,128)S(1)}, f32[1,8,3,256]{3,1,2,0:T(8,128)}, u32[]{:S(2)}) %copy-start.5) | copy-done | bytes 24600
  5.0 0.0 copy-start.3
  5.0 0.0 copy-start.4
  5.0 56.0 %render_step.1 = (f32[1024,128]{1,0:T(8,128)S(1)}, f32[59,128]{1,0:T(8,128)S(1)}, f32[59,128]{1,0:T(8,128)S(1)}) custom-call(f32[59,1024]{1,0:T(8,128)S(1)} %copy-done, s32[2,32]{1,0:T(2,128)S(1)} %bitcast.7, s32[1,32]{1,0:T(1,128)S(1)} %copy-done.7, s32[1,32]{1,0:T(1,128)S(1)} %copy-done.8, s32[1,32]{1,0:T(1,128)S(1)} %copy-done.9, ...), custom_call_target="tpu_custom_call" | custom-call | tf_op jit(solution)/shard_map/render_step/pallas_call | solution.py:781
  61.0 0.0 copy-done.3
  61.0 0.0 copy-done.4
  61.0 1.1 %adam.1 = (f32[59,1024]{1,0:T(8,128)}, f32[59,1024]{1,0:T(8,128)}, f32[59,1024]{1,0:T(8,128)}, f32[59,1024]{1,0:T(8,128)}) custom-call(f32[1024,128]{1,0:T(8,128)S(1)} %get-tuple-element.7.grads_ref, f32[59,128]{1,0:T(8,128)S(1)} %get-tuple-element.8.from_left_ref, f32[59,128]{1,0:T(8,128)S(1)} %get-tuple-element.9.from_right_ref, f32[59,1024]{1,0:T(8,128)S(1)} %copy-done, ...), custom_call_target="tpu_custom_call" | custom-call | tf_op jit(solution)/shard_map/adam/pallas_call | solution.py:861
Async XLA Ops:
  0.6 0.7 %copy-start.8 = (s32[1,32]{1,0:T(1,128)S(1)}, s32[1,32]{1,0:T(1,128)}, u32[]{:S(2)}) copy-start(s32[1,32]{1,0:T(1,128)} %owner_hbm.1) | copy-start | bytes 388
  0.6 0.7 %copy-start.9 = (s32[1,32]{1,0:T(1,128)S(1)}, s32[1,32]{1,0:T(1,128)}, u32[]{:S(2)}) copy-start(s32[1,32]{1,0:T(1,128)} %cell_hbm.1) | copy-start | bytes 388
  0.7 0.7 %copy-start.10 = (f32[3]{0:T(128)S(1)}, f32[3]{0:T(128)}, u32[]{:S(2)}) copy-start(f32[3]{0:T(128)} %background_hbm.1) | copy-start | bytes 40
  0.7 0.7 %copy-start.6 = (s32[1,32,2]{1,2,0:T(2,128)S(1)}, s32[1,32,2]{1,2,0:T(2,128)}, u32[]{:S(2)}) copy-start(s32[1,32,2]{1,2,0:T(2,128)} %param.14) | copy-start | bytes 772
  0.7 0.7 %copy-start.7 = (s32[1,32]{1,0:T(1,128)S(1)}, s32[1,32]{1,0:T(1,128)}, u32[]{:S(2)}) copy-start(s32[1,32]{1,0:T(1,128)} %live_hbm.1) | copy-start | bytes 388
  1.4 1.0 %copy-start = (f32[59,1024]{1,0:T(8,128)S(1)}, f32[59,1024]{1,0:T(8,128)}, u32[]{:S(2)}) copy-start(f32[59,1024]{1,0:T(8,128)} %params_ref.1) | copy-start | bytes 724996
  2.3 1.0 %copy-start.1 = (bf16[32,32,256]{2,1,0:T(8,128)(2,1)S(1)}, bf16[32,32,256]{2,1,0:T(8,128)(2,1)}, u32[]{:S(2)}) copy-start(bf16[32,32,256]{2,1,0:T(8,128)(2,1)} %constant.4.clone.features_hbm) | copy-start | bytes 1572868
  3.4 0.9 %copy-start.2 = (bf16[32,16,256]{2,1,0:T(8,128)(2,1)S(1)}, bf16[32,16,256]{2,1,0:T(8,128)(2,1)}, u32[]{:S(2)}) copy-start(bf16[32,16,256]{2,1,0:T(8,128)(2,1)} %constant.5.clone.moments_hbm) | copy-start | bytes 786436
  4.3 0.7 %copy-start.5 = (f32[1,8,3,256]{3,1,2,0:T(8,128)S(1)}, f32[1,8,3,256]{3,1,2,0:T(8,128)}, u32[]{:S(2)}) copy-start(f32[1,8,3,256]{3,1,2,0:T(8,128)} %param.18) | copy-start | bytes 73732
  5.0 56.0 %copy-start.3 = (f32[59,1024]{1,0:T(8,128)S(1)}, f32[59,1024]{1,0:T(8,128)}, u32[]{:S(2)}) copy-start(f32[59,1024]{1,0:T(8,128)} %first_ref.1) | copy-start | bytes 724996
  5.0 56.0 %copy-start.4 = (f32[59,1024]{1,0:T(8,128)S(1)}, f32[59,1024]{1,0:T(8,128)}, u32[]{:S(2)}) copy-start(f32[59,1024]{1,0:T(8,128)} %second_ref.1) | copy-start | bytes 724996

commit v3 on v2

--- a/solution.py
+++ b/solution.py
@@ -1,3 +1,4 @@
+import functools
 import math
 
 import jax
@@ -27,12 +28,15 @@
 PLANES = 16
 ROWS = 64
 COLS = 96
-UNROLL = 4
+UNROLL = 8
+START_UNROLL = 1
 HALVES = 2
 WIDE = PIX // HALVES
 LOW = BLOCKS
 HIGH = BLOCKS + 1
 DEAD = POOL
+FROM_LEFT = 2 * SUB
+FROM_RIGHT = FROM_LEFT + 1
 ORIGIN_X = 64.0
 ORIGIN_Y = 32.0
 
@@ -63,7 +67,7 @@
 f32 = jnp.float32
 bf16 = jnp.bfloat16
 MESH = pl.DeviceIdType.MESH
-VMEM_LIMIT = 32 * 1024 * 1024
+VMEM_LIMIT = 60 * 1024 * 1024
 
 
 def pixel_monomials():
@@ -389,11 +393,13 @@
                 ahead = ahead + alphas[t] * gap
             parts[j] = split(jnp.concatenate(gradients, axis=0), 2)
             parts[j] += split(jnp.concatenate(weights, axis=0), 2)
+        both = [jnp.concatenate([parts[0][k], parts[1][k]], axis=0) for k in range(4)]
         total = None
-        for k in range(4):
+        for k in range(2):
+            rows = (for_gradient, for_weight)[k]
             term = lax.dot_general(
-                (for_gradient, for_weight)[k // 2],
-                jnp.concatenate([parts[0][k], parts[1][k]], axis=0),
+                jnp.concatenate([rows, rows], axis=1),
+                jnp.concatenate(both[2 * k : 2 * k + 2], axis=1),
                 (((1,), (1,)), ((), ())),
                 preferred_element_type=f32,
             )
@@ -557,8 +563,6 @@
     features_hbm,
     moments_hbm,
     grads_ref,
-    from_left,
-    from_right,
     blocks,
     live,
     background,
@@ -649,31 +653,39 @@
             src_ref=src, dst_ref=dst, send_sem=send, recv_sem=recv, device_id=where, device_id_type=MESH
         )
 
-    def label(d):
-        where = lax.rem(me + d, count)
-        return remote(labels.at[d], got_labels.at[d], label_send.at[d], label_recv.at[d], dom=where)
-
-    def message(d):
-        return pl.ds(pl.multiple_of(d * MESSAGE, MESSAGE), MESSAGE)
-
-    def payload(h, d):
-        where = lax.rem(me + d, count)
-        rows = message(d)
-        return remote(sent.at[h, rows], got.at[h, rows], send_sem.at[h, d], recv_sem.at[h, d], dom=where)
-
-    def reply(h, d):
-        where = lax.rem(me + count - d, count)
-        rows = message(d)
+    def label(d, many=1):
+        rows = pl.ds(d, many)
         return remote(
-            replies.at[h, rows], answers.at[h, rows], reply_send.at[h, d], reply_recv.at[h, d], dom=where
-        )
-
-    def for_all(act):
+            labels.at[rows], got_labels.at[rows], label_send, label_recv, dom=lax.rem(me + d, count)
+        )
+
+    def message(d, many):
+        return pl.ds(pl.multiple_of(d * MESSAGE, MESSAGE), many * MESSAGE)
+
+    def payload(h, d, many=1):
+        rows = message(d, many)
+        return remote(
+            sent.at[h, rows], got.at[h, rows], send_sem.at[h], recv_sem.at[h], dom=lax.rem(me + d, count)
+        )
+
+    def reply(h, d, many=1):
+        rows = message(d, many)
+        return remote(
+            replies.at[h, rows],
+            answers.at[h, rows],
+            reply_send.at[h],
+            reply_recv.at[h],
+            dom=lax.rem(me + count - d, count),
+        )
+
+    def start_all(copy):
         def one(d, carry):
-            act(d)
+            copy(d).start()
             return carry
 
-        lax.fori_loop(1, count, one, 0)
+        lax.fori_loop(1, count, one, 0, unroll=START_UNROLL)
+
+    others = count - 1
 
     halo = [
         remote(
@@ -693,7 +705,7 @@
     ]
     for copy in halo:
         copy.start()
-    for_all(lambda d: label(d).start())
+    start_all(label)
     got_labels[0] = labels[0]
 
     for copy in own:
@@ -715,12 +727,12 @@
         rendered = [pieces[r * PIECES : (r + 1) * PIECES, :] for r in range(PARTS)]
         rendered = jnp.concatenate(rendered, axis=1)
         put_slots(sent.at[h], exact_pick(pack, rendered))
-        for_all(lambda d: payload(h, d).start())
+        start_all(functools.partial(payload, h))
         got[h, :MESSAGE] = sent[h, :MESSAGE]
 
     for copy in later:
         copy.wait()
-    for_all(lambda d: label(d).wait())
+    label(1, others).wait()
     arrived = jnp.concatenate([got_labels[d] for d in range(32)], axis=0)
     arrived_col = jnp.concatenate([arrived[:, 0:1], arrived[:, 1:2]], axis=0)
     arrived_row = to_row(arrived_col)
@@ -735,14 +747,14 @@
     scatter = jnp.where(scatter, 1.0, 0.0)
     colours = [background[c] for c in range(3)]
     for h in range(HALVES):
-        for_all(lambda d: payload(h, d).wait())
+        payload(h, 1, others).wait()
         grid = exact_pick(gather, get_slots(got.at[h]))
         put_slots(replies.at[h], exact_pick(scatter, composite(h, grid, target, colours)))
-        for_all(lambda d: reply(h, d).start())
+        start_all(functools.partial(reply, h))
         answers[h, :MESSAGE] = replies[h, :MESSAGE]
 
     for h in range(HALVES):
-        for_all(lambda d: reply(h, d).wait())
+        reply(h, 1, others).wait()
         back = exact_pick(unpack, get_slots(answers.at[h]))
         for k in range(WIDE // BLOCK):
             for c in range(SUB):
@@ -757,8 +769,8 @@
     gather_moments(rows[0:1], rows[1:2], moved, summed)
     pull_splat(1, pool, summed, grads_ref)
     edges = [
-        remote(block_rows_of(grads_ref, HIGH), from_left, edge_send.at[0], edge_recv.at[0], region=upper),
-        remote(block_rows_of(grads_ref, LOW), from_right, edge_send.at[1], edge_recv.at[1], region=lower),
+        remote(block_rows_of(grads_ref, HIGH), block_rows_of(grads_ref, FROM_LEFT), edge_send.at[0], edge_recv.at[0], region=upper),
+        remote(block_rows_of(grads_ref, LOW), block_rows_of(grads_ref, FROM_RIGHT), edge_send.at[1], edge_recv.at[1], region=lower),
     ]
     for copy in edges:
         copy.start()
@@ -780,13 +792,9 @@
     label = vmem((32, 1, BLOCK), f32)
     return pl.pallas_call(
         step_kernel,
-        out_shape=(
-            shape((2 * SUB * ROWS, BLOCK), f32),
-            shape((PARAMS, BLOCK), f32),
-            shape((PARAMS, BLOCK), f32),
-        ),
-        in_specs=[whole(pl.ANY)] * 9,
-        out_specs=(whole(),) * 3,
+        out_shape=shape(((FROM_RIGHT + 1) * ROWS, BLOCK), f32),
+        in_specs=[whole(pltpu.HBM)] * 9,
+        out_specs=whole(),
         scratch_shapes=[
             smem((2, PIECES), jnp.int32),
             smem((1, PIECES), jnp.int32),
@@ -819,12 +827,12 @@
             dma((2,)),
             dma((2,)),
             dma((2,)),
-            dma((32,)),
-            dma((32,)),
-            dma((HALVES, 32)),
-            dma((HALVES, 32)),
-            dma((HALVES, 32)),
-            dma((HALVES, 32)),
+            dma,
+            dma,
+            dma((HALVES,)),
+            dma((HALVES,)),
+            dma((HALVES,)),
+            dma((HALVES,)),
         ],
         compiler_params=pltpu.CompilerParams(
             collective_id=0, has_side_effects=True, vmem_limit_bytes=VMEM_LIMIT
@@ -834,16 +842,16 @@
 
 
 def adam_kernel(
-    grads_ref, from_left_ref, from_right_ref, params_ref, first_ref, second_ref,
+    grads_ref, params_ref, first_ref, second_ref,
     gradient_ref, new_params_ref, new_first_ref, new_second_ref,
 ):
     for b in range(BLOCKS):
         cols = slice(b * BLOCK, (b + 1) * BLOCK)
         gradient = grads_ref[b * ROWS : b * ROWS + PARAMS, :]
         if b == 0:
-            gradient = gradient + from_left_ref[...]
+            gradient = gradient + grads_ref[FROM_LEFT * ROWS : FROM_LEFT * ROWS + PARAMS, :]
         if b == BLOCKS - 1:
-            gradient = gradient + from_right_ref[...]
+            gradient = gradient + grads_ref[FROM_RIGHT * ROWS : FROM_RIGHT * ROWS + PARAMS, :]
         new_first = beta_one * first_ref[:, cols] + (1 - beta_one) * gradient
         new_second = beta_two * second_ref[:, cols] + (1 - beta_two) * gradient * gradient
         update = (
@@ -861,7 +869,7 @@
     return pl.pallas_call(
         adam_kernel,
         out_shape=(jax.ShapeDtypeStruct((PARAMS, BLOCKS * BLOCK), f32),) * 4,
-        in_specs=[whole()] * 6,
+        in_specs=[whole()] * 4,
         out_specs=(whole(),) * 4,
         compiler_params=pltpu.CompilerParams(vmem_limit_bytes=8 * 1024 * 1024),
         name="adam",
@@ -879,7 +887,7 @@
     target,
     background,
 ):
-    grads, from_left, from_right = step(
+    grads = step(
         params,
         piece_blocks[0].T,
         piece_live,
@@ -890,7 +898,7 @@
         jnp.asarray(exponent_features()),
         jnp.asarray(moment_features()),
     )
-    return adam(grads, from_left, from_right, params, first_moment, second_moment)
+    return adam(grads, params, first_moment, second_moment)
 
 
 def solution(mesh):

time: 62.4 us -> 52.7 us (0.84)
  Pallas kernels: 57.1 us -> 50.8 us
  local copies, waits for them, and re-layouts: 4.37 us -> 1.07 us
    pallas_call x1, Pallas kernels: 56 us -> 49.7 us  [step(): pl.pallas_call(step_kernel, out_shape=shape(((FROM_RIGHT + 1) * ROWS, BLO...]
    unnamed x22 -> x8, local copies, waits for them, and re-layouts: 4.37 us -> 1.07 us
where the time goes in v3:
time: 52.7 us; the launch traced here: 52.6 us
  Pallas kernels  50.8 us (96%)
  local copies, waits for them, and re-layouts  1.07 us (2%)
  between operations  0.7 us (1%)
    pallas_call x1, Pallas kernels, step(): pl.pallas_call(step_kernel, out_shape=shape(((FROM_RIGHT + 1) * ROWS, BLO...  49.7 us
    pallas_call x1, Pallas kernels, adam(): pl.pallas_call(adam_kernel, out_shape=(jax.ShapeDtypeStruct((PARAMS, BLOC...  1.1 us
    unnamed x8, local copies, waits for them, and re-layouts  1.07 us

profile of v3, /device:TPU:1, one launch (start us, length us, event | category | flops | bytes accessed | tf_op | source)
XLA Modules:
  0.0 52.6 jit_solution(11830135840832718598)
XLA Ops:
  0.6 0.0 copy-start.1
  0.6 0.0 copy-start.2
  0.7 0.0 copy-start.3
  0.7 49.7 %render_step.1.grads_ref = f32[1152,128]{1,0:T(8,128)} custom-call(f32[59,1024]{1,0:T(8,128)} %params_ref.1, s32[2,32]{1,0:T(2,128)} %bitcast.7, s32[1,32]{1,0:T(1,128)} %live_hbm.1, s32[1,32]{1,0:T(1,128)} %owner_hbm.1, s32[1,32]{1,0:T(1,128)} %cell_hbm.1, f32[3,8,256]{2,1,0:T(8,128)} %bitcast.6, f32[3]{0:T(128)} %background_hbm.1, ...), custom_call_target="tpu_custom_call" | custom-call | tf_op jit(solution)/shard_map/render_step/pallas_call | solution.py:793
  50.4 0.0 copy-done.1
  50.4 0.0 copy-done.2
  50.4 0.0 copy-done.3
  50.4 0.0 copy-start
  50.4 1.1 %copy-done = f32[1152,128]{1,0:T(8,128)S(1)} copy-done((f32[1152,128]{1,0:T(8,128)S(1)}, f32[1152,128]{1,0:T(8,128)}, u32[]{:S(2)}) %copy-start) | copy-done | bytes 589848
  51.5 1.1 %adam.1 = (f32[59,1024]{1,0:T(8,128)}, f32[59,1024]{1,0:T(8,128)}, f32[59,1024]{1,0:T(8,128)}, f32[59,1024]{1,0:T(8,128)}) custom-call(f32[1152,128]{1,0:T(8,128)S(1)} %copy-done, f32[59,1024]{1,0:T(8,128)S(1)} %copy-done.1, f32[59,1024]{1,0:T(8,128)S(1)} %copy-done.2, f32[59,1024]{1,0:T(8,128)S(1)} %copy-done.3), custom_call_target="tpu_custom_call" | custom-call | tf_op jit(solution)/shard_map/adam/pallas_call | solution.py:869
Async XLA Ops:
  0.6 49.8 %copy-start.1 = (f32[59,1024]{1,0:T(8,128)S(1)}, f32[59,1024]{1,0:T(8,128)}, u32[]{:S(2)}) copy-start(f32[59,1024]{1,0:T(8,128)} %params_ref.1) | copy-start | bytes 724996
  0.6 49.8 %copy-start.2 = (f32[59,1024]{1,0:T(8,128)S(1)}, f32[59,1024]{1,0:T(8,128)}, u32[]{:S(2)}) copy-start(f32[59,1024]{1,0:T(8,128)} %first_ref.1) | copy-start | bytes 724996
  0.7 49.8 %copy-start.3 = (f32[59,1024]{1,0:T(8,128)S(1)}, f32[59,1024]{1,0:T(8,128)}, u32[]{:S(2)}) copy-start(f32[59,1024]{1,0:T(8,128)} %second_ref.1) | copy-start | bytes 724996
  50.4 1.1 %copy-start = (f32[1152,128]{1,0:T(8,128)S(1)}, f32[1152,128]{1,0:T(8,128)}, u32[]{:S(2)}) copy-start(f32[1152,128]{1,0:T(8,128)} %render_step.1.grads_ref) | copy-start | bytes 1769476

commit v4 on v3

--- a/solution.py
+++ b/solution.py
@@ -29,6 +29,7 @@
 ROWS = 64
 COLS = 96
 UNROLL = 8
+MIDDLE_UNROLL = 4
 START_UNROLL = 1
 HALVES = 2
 WIDE = PIX // HALVES
@@ -293,7 +294,9 @@
     return first, second
 
 
-def forward_half(h, blocks, live, features_ref, table, spread, prefix_ref, segment_ref, pieces):
+def forward_half(
+    h, blocks, live, features_ref, table, spread, prefix_ref, segment_ref, pieces, alphas_ref
+):
     sub = iota((SUB, WIDE), 0)
 
     def piece(p, carry):
@@ -306,7 +309,9 @@
             sums = [jnp.zeros((SUB, WIDE), f32) for _ in range(3)]
             for t in range(STEPS):
                 rows = slice(t * SUB, (t + 1) * SUB)
-                weight = jnp.exp2(exponent[rows]) * transmit
+                alpha = jnp.exp2(exponent[rows])
+                alphas_ref[h, p, j, rows] = alpha
+                weight = alpha * transmit
                 transmit = transmit - weight
                 for c in range(3):
                     tone = spread[block, c, rows, :]
@@ -336,8 +341,29 @@
     lax.fori_loop(0, PIECES, piece, 0, unroll=UNROLL)
 
 
+def weigh_half(h, prefix_ref, alphas_ref, weights_ref, ends_ref, weight_parts_ref):
+    def piece(p, carry):
+        for j in range(2):
+            transmit = prefix_ref[h, p, j]
+            weights = []
+            for t in range(STEPS):
+                rows = slice(t * SUB, (t + 1) * SUB)
+                weight = alphas_ref[h, p, j, rows] * transmit
+                transmit = transmit - weight
+                weights_ref[h, p, j, rows] = weight
+                weights.append(weight)
+            ends_ref[h, p, j] = transmit
+            weight_parts_ref[h, p, j * BLOCK : (j + 1) * BLOCK] = jnp.concatenate(
+                split(jnp.concatenate(weights, axis=0), 2), axis=1
+            )
+        return carry
+
+    lax.fori_loop(0, PIECES, piece, 0, unroll=MIDDLE_UNROLL)
+
+
 def backward_half(
-    h, blocks, live, features_ref, moments_ref, table, prefix_ref, segment_ref, cotangent, moved
+    h, blocks, live, moments_ref, table, segment_ref, alphas_ref, weights_ref, ends_ref, weight_parts_ref,
+    cotangent, moved,
 ):
     sub = iota((SUB, WIDE), 0)
     nothing = jnp.zeros((16, WIDE), bf16)
@@ -345,7 +371,6 @@
     lanes = slice(h * WIDE, (h + 1) * WIDE)
 
     def piece(p, carry):
-        features = features_ref[p, :, lanes]
         monomials = moments_ref[p, :, lanes]
         cot = jnp.concatenate(
             [
@@ -362,44 +387,35 @@
         for_weight = jnp.concatenate([nothing, colour_rows], axis=0)
         state = []
         for j, block in enumerate(two_blocks(p, blocks, live)):
-            exponent = exponents(table, features, block)
             tone = jnp.dot(table[block], tones, preferred_element_type=f32)
-            transmit = prefix_ref[h, p, j]
-            alphas, weights = [], []
-            for t in range(STEPS):
-                alpha = jnp.exp2(exponent[t * SUB : (t + 1) * SUB])
-                weight = alpha * transmit
-                transmit = transmit - weight
-                alphas.append(alpha)
-                weights.append(weight)
             seen = segment_ref[h, p, j, 0] * cot[0:1]
             for c in (1, 2):
                 seen = seen + segment_ref[h, p, j, c] * cot[c : c + 1]
             run = seen
             for shift in (1, 2, 4):
                 run = run + jnp.where(sub < SUB - shift, roll_rows(run, -shift), 0.0)
-            state.append((tone, transmit, alphas, weights, run))
-        behind = state[1][1][SUB - 1 :, :] * cot[3:4]
+            state.append((tone, run))
+        behind = ends_ref[h, p, 1, SUB - 1 :, :] * cot[3:4]
         parts = [None, None]
         for j in (1, 0):
-            tone, transmit, alphas, weights, run = state[j]
+            tone, run = state[j]
             after = jnp.where(sub < SUB - 1, roll_rows(run, -1), 0.0) + behind
             behind = behind + run[0:1]
-            ahead = after / transmit
+            ahead = after / ends_ref[h, p, j]
             gradients = [None] * STEPS
             for t in reversed(range(STEPS)):
-                gap = tone[t * SUB : (t + 1) * SUB] - ahead
-                gradients[t] = weights[t] * gap
-                ahead = ahead + alphas[t] * gap
-            parts[j] = split(jnp.concatenate(gradients, axis=0), 2)
-            parts[j] += split(jnp.concatenate(weights, axis=0), 2)
-        both = [jnp.concatenate([parts[0][k], parts[1][k]], axis=0) for k in range(4)]
+                rows = slice(t * SUB, (t + 1) * SUB)
+                gap = tone[rows] - ahead
+                gradients[t] = weights_ref[h, p, j, rows] * gap
+                ahead = ahead + alphas_ref[h, p, j, rows] * gap
+            parts[j] = jnp.concatenate(split(jnp.concatenate(gradients, axis=0), 2), axis=1)
+        both = [jnp.concatenate(parts, axis=0), weight_parts_ref[h, p]]
         total = None
         for k in range(2):
             rows = (for_gradient, for_weight)[k]
             term = lax.dot_general(
                 jnp.concatenate([rows, rows], axis=1),
-                jnp.concatenate(both[2 * k : 2 * k + 2], axis=1),
+                both[k],
                 (((1,), (1,)), ((), ())),
                 preferred_element_type=f32,
             )
@@ -579,6 +595,10 @@
     spread,
     prefix,
     segment,
+    alphas,
+    weights,
+    ends,
+    weight_parts,
     pieces,
     sent,
     got,
@@ -723,13 +743,14 @@
     for copy in scalars:
         copy.wait()
     for h in range(HALVES):
-        forward_half(h, blocks, live, features, table, spread, prefix, segment, pieces)
+        forward_half(h, blocks, live, features, table, spread, prefix, segment, pieces, alphas)
         rendered = [pieces[r * PIECES : (r + 1) * PIECES, :] for r in range(PARTS)]
         rendered = jnp.concatenate(rendered, axis=1)
         put_slots(sent.at[h], exact_pick(pack, rendered))
         start_all(functools.partial(payload, h))
         got[h, :MESSAGE] = sent[h, :MESSAGE]
 
+    weigh_half(0, prefix, alphas, weights, ends, weight_parts)
     for copy in later:
         copy.wait()
     label(1, others).wait()
@@ -752,6 +773,8 @@
         put_slots(replies.at[h], exact_pick(scatter, composite(h, grid, target, colours)))
         start_all(functools.partial(reply, h))
         answers[h, :MESSAGE] = replies[h, :MESSAGE]
+        if h + 1 < HALVES:
+            weigh_half(h + 1, prefix, alphas, weights, ends, weight_parts)
 
     for h in range(HALVES):
         reply(h, 1, others).wait()
@@ -762,7 +785,7 @@
                 rows = back[:, lanes] if c < 4 else jnp.zeros((PIECES, BLOCK), f32)
                 cotangent[pl.ds(k * PIECES * SUB + c, PIECES, stride=SUB), :] = rows
         backward_half(
-            h, blocks, live, features, moments, table, prefix, segment, cotangent, moved
+            h, blocks, live, moments, table, segment, alphas, weights, ends, weight_parts, cotangent, moved
         )
 
     rows = own_block(block_rows[...]).astype(f32)
@@ -812,6 +835,10 @@
             vmem((TAB, 3, BLOCK, BLOCK), f32),
             vmem((HALVES, PIECES, 2, SUB, WIDE), f32),
             vmem((HALVES, PIECES, 2, 3, SUB, WIDE), f32),
+            vmem((HALVES, PIECES, 2, BLOCK, WIDE), f32),
+            vmem((HALVES, PIECES, 2, BLOCK, WIDE), f32),
+            vmem((HALVES, PIECES, 2, SUB, WIDE), f32),
+            vmem((HALVES, PIECES, 2 * BLOCK, 2 * WIDE), bf16),
             vmem((4 * WIDE // BLOCK * PIECES, BLOCK), f32),
             slots,
             slots,

time: 52.7 us -> 50.7 us (0.962)
  Pallas kernels: 50.8 us -> 48.8 us
    pallas_call x1, Pallas kernels: 49.7 us -> 47.7 us  [step(): pl.pallas_call(step_kernel, out_shape=shape(((FROM_RIGHT + 1) * ROWS, BLO...]
where the time goes in v4:
time: 50.7 us; the launch traced here: 50.5 us
  Pallas kernels  48.8 us (96%)
  local copies, waits for them, and re-layouts  1.07 us (2%)
  between operations  0.7 us (1%)
    pallas_call x1, Pallas kernels, step(): pl.pallas_call(step_kernel, out_shape=shape(((FROM_RIGHT + 1) * ROWS, BLO...  47.7 us
    pallas_call x1, Pallas kernels, adam(): pl.pallas_call(adam_kernel, out_shape=(jax.ShapeDtypeStruct((PARAMS, BLOC...  1.1 us
    unnamed x8, local copies, waits for them, and re-layouts  1.07 us

profile of v4, /device:TPU:1, one launch (start us, length us, event | category | flops | bytes accessed | tf_op | source)
XLA Modules:
  0.0 50.5 jit_solution(10867855693649982420)
XLA Ops:
  0.6 0.0 copy-start.1
  0.6 0.0 copy-start.2
  0.7 0.0 copy-start.3
  0.7 47.7 %render_step.1.grads_ref = f32[1152,128]{1,0:T(8,128)} custom-call(f32[59,1024]{1,0:T(8,128)} %params_ref.1, s32[2,32]{1,0:T(2,128)} %bitcast.7, s32[1,32]{1,0:T(1,128)} %live_hbm.1, s32[1,32]{1,0:T(1,128)} %owner_hbm.1, s32[1,32]{1,0:T(1,128)} %cell_hbm.1, f32[3,8,256]{2,1,0:T(8,128)} %bitcast.6, f32[3]{0:T(128)} %background_hbm.1, ...), custom_call_target="tpu_custom_call" | custom-call | tf_op jit(solution)/shard_map/render_step/pallas_call | solution.py:816
  48.3 0.0 copy-done.1
  48.4 0.0 copy-done.2
  48.4 0.0 copy-done.3
  48.4 0.0 copy-start
  48.4 1.1 %copy-done = f32[1152,128]{1,0:T(8,128)S(1)} copy-done((f32[1152,128]{1,0:T(8,128)S(1)}, f32[1152,128]{1,0:T(8,128)}, u32[]{:S(2)}) %copy-start) | copy-done | bytes 589848
  49.4 1.1 %adam.1 = (f32[59,1024]{1,0:T(8,128)}, f32[59,1024]{1,0:T(8,128)}, f32[59,1024]{1,0:T(8,128)}, f32[59,1024]{1,0:T(8,128)}) custom-call(f32[1152,128]{1,0:T(8,128)S(1)} %copy-done, f32[59,1024]{1,0:T(8,128)S(1)} %copy-done.1, f32[59,1024]{1,0:T(8,128)S(1)} %copy-done.2, f32[59,1024]{1,0:T(8,128)S(1)} %copy-done.3), custom_call_target="tpu_custom_call" | custom-call | tf_op jit(solution)/shard_map/adam/pallas_call | solution.py:896
Async XLA Ops:
  0.6 47.7 %copy-start.1 = (f32[59,1024]{1,0:T(8,128)S(1)}, f32[59,1024]{1,0:T(8,128)}, u32[]{:S(2)}) copy-start(f32[59,1024]{1,0:T(8,128)} %params_ref.1) | copy-start | bytes 724996
  0.6 47.7 %copy-start.2 = (f32[59,1024]{1,0:T(8,128)S(1)}, f32[59,1024]{1,0:T(8,128)}, u32[]{:S(2)}) copy-start(f32[59,1024]{1,0:T(8,128)} %first_ref.1) | copy-start | bytes 724996
  0.7 47.7 %copy-start.3 = (f32[59,1024]{1,0:T(8,128)S(1)}, f32[59,1024]{1,0:T(8,128)}, u32[]{:S(2)}) copy-start(f32[59,1024]{1,0:T(8,128)} %second_ref.1) | copy-start | bytes 724996
  48.4 1.1 %copy-start = (f32[1152,128]{1,0:T(8,128)S(1)}, f32[1152,128]{1,0:T(8,128)}, u32[]{:S(2)}) copy-start(f32[1152,128]{1,0:T(8,128)} %render_step.1.grads_ref) | copy-start | bytes 1769476

commit v5 on v4

--- a/solution.py
+++ b/solution.py
@@ -28,7 +28,7 @@
 PLANES = 16
 ROWS = 64
 COLS = 96
-UNROLL = 8
+UNROLL = 16
 MIDDLE_UNROLL = 4
 START_UNROLL = 1
 HALVES = 2
@@ -700,7 +700,7 @@
 
     def start_all(copy):
         def one(d, carry):
-            copy(d).start()
+            copy(count - d).start()
             return carry
 
         lax.fori_loop(1, count, one, 0, unroll=START_UNROLL)
@@ -725,14 +725,14 @@
     ]
     for copy in halo:
         copy.start()
-    start_all(label)
-    got_labels[0] = labels[0]
 
     for copy in own:
         copy.wait()
     for b in range(POOL, 2 * SUB):
         pool[b * ROWS : b * ROWS + PARAMS, :] = pool[0:PARAMS, :]
     tabulate(0, SUB, pool, stage, turned, table, spread)
+    start_all(label)
+    got_labels[0] = labels[0]
     for copy in halo:
         copy.wait_recv()
     tabulate(1, POOL - SUB, pool, stage, turned, table, spread)

time: 50.7 us -> 48.4 us (0.955)
  Pallas kernels: 48.8 us -> 46.5 us
    pallas_call x1, Pallas kernels: 47.7 us -> 45.4 us  [step(): pl.pallas_call(step_kernel, out_shape=shape(((FROM_RIGHT + 1) * ROWS, BLO...]
where the time goes in v5:
time: 48.4 us; the launch traced here: 48.3 us
  Pallas kernels  46.5 us (96%)
  local copies, waits for them, and re-layouts  1.07 us (2%)
  between operations  0.7 us (1%)
    pallas_call x1, Pallas kernels, step(): pl.pallas_call(step_kernel, out_shape=shape(((FROM_RIGHT + 1) * ROWS, BLO...  45.4 us
    pallas_call x1, Pallas kernels, adam(): pl.pallas_call(adam_kernel, out_shape=(jax.ShapeDtypeStruct((PARAMS, BLOC...  1.1 us
    unnamed x8, local copies, waits for them, and re-layouts  1.07 us

profile of v5, /device:TPU:1, one launch (start us, length us, event | category | flops | bytes accessed | tf_op | source)
XLA Modules:
  0.0 48.3 jit_solution(13387296186729831811)
XLA Ops:
  0.6 0.0 copy-start.1
  0.6 0.0 copy-start.2
  0.7 0.0 copy-start.3
  0.7 45.4 %render_step.1.grads_ref = f32[1152,128]{1,0:T(8,128)} custom-call(f32[59,1024]{1,0:T(8,128)} %params_ref.1, s32[2,32]{1,0:T(2,128)} %bitcast.7, s32[1,32]{1,0:T(1,128)} %live_hbm.1, s32[1,32]{1,0:T(1,128)} %owner_hbm.1, s32[1,32]{1,0:T(1,128)} %cell_hbm.1, f32[3,8,256]{2,1,0:T(8,128)} %bitcast.6, f32[3]{0:T(128)} %background_hbm.1, ...), custom_call_target="tpu_custom_call" | custom-call | tf_op jit(solution)/shard_map/render_step/pallas_call | solution.py:816
  46.1 0.0 copy-done.1
  46.1 0.0 copy-done.2
  46.1 0.0 copy-done.3
  46.1 0.0 copy-start
  46.1 1.1 %copy-done = f32[1152,128]{1,0:T(8,128)S(1)} copy-done((f32[1152,128]{1,0:T(8,128)S(1)}, f32[1152,128]{1,0:T(8,128)}, u32[]{:S(2)}) %copy-start) | copy-done | bytes 589848
  47.2 1.1 %adam.1 = (f32[59,1024]{1,0:T(8,128)}, f32[59,1024]{1,0:T(8,128)}, f32[59,1024]{1,0:T(8,128)}, f32[59,1024]{1,0:T(8,128)}) custom-call(f32[1152,128]{1,0:T(8,128)S(1)} %copy-done, f32[59,1024]{1,0:T(8,128)S(1)} %copy-done.1, f32[59,1024]{1,0:T(8,128)S(1)} %copy-done.2, f32[59,1024]{1,0:T(8,128)S(1)} %copy-done.3), custom_call_target="tpu_custom_call" | custom-call | tf_op jit(solution)/shard_map/adam/pallas_call | solution.py:896
Async XLA Ops:
  0.6 45.5 %copy-start.1 = (f32[59,1024]{1,0:T(8,128)S(1)}, f32[59,1024]{1,0:T(8,128)}, u32[]{:S(2)}) copy-start(f32[59,1024]{1,0:T(8,128)} %params_ref.1) | copy-start | bytes 724996
  0.6 45.5 %copy-start.2 = (f32[59,1024]{1,0:T(8,128)S(1)}, f32[59,1024]{1,0:T(8,128)}, u32[]{:S(2)}) copy-start(f32[59,1024]{1,0:T(8,128)} %first_ref.1) | copy-start | bytes 724996
  0.7 45.5 %copy-start.3 = (f32[59,1024]{1,0:T(8,128)S(1)}, f32[59,1024]{1,0:T(8,128)}, u32[]{:S(2)}) copy-start(f32[59,1024]{1,0:T(8,128)} %second_ref.1) | copy-start | bytes 724996
  46.1 1.1 %copy-start = (f32[1152,128]{1,0:T(8,128)S(1)}, f32[1152,128]{1,0:T(8,128)}, u32[]{:S(2)}) copy-start(f32[1152,128]{1,0:T(8,128)} %render_step.1.grads_ref) | copy-start | bytes 1769476

commit v6 on v5

--- a/solution.py
+++ b/solution.py
@@ -698,9 +698,9 @@
             dom=lax.rem(me + count - d, count),
         )
 
-    def start_all(copy):
+    def start_all(copy, falling=True):
         def one(d, carry):
-            copy(count - d).start()
+            copy(count - d if falling else d).start()
             return carry
 
         lax.fori_loop(1, count, one, 0, unroll=START_UNROLL)
@@ -771,7 +771,7 @@
         payload(h, 1, others).wait()
         grid = exact_pick(gather, get_slots(got.at[h]))
         put_slots(replies.at[h], exact_pick(scatter, composite(h, grid, target, colours)))
-        start_all(functools.partial(reply, h))
+        start_all(functools.partial(reply, h), falling=False)
         answers[h, :MESSAGE] = replies[h, :MESSAGE]
         if h + 1 < HALVES:
             weigh_half(h + 1, prefix, alphas, weights, ends, weight_parts)

time: 48.4 us -> 49.1 us (1.014)
  Pallas kernels: 46.5 us -> 47.2 us
    pallas_call x1, Pallas kernels: 45.4 us -> 46.1 us  [step(): pl.pallas_call(step_kernel, out_shape=shape(((FROM_RIGHT + 1) * ROWS, BLO...]
where the time goes in v6:
time: 49.1 us; the launch traced here: 49 us
  Pallas kernels  47.2 us (96%)
  local copies, waits for them, and re-layouts  1.07 us (2%)
  between operations  0.7 us (1%)
    pallas_call x1, Pallas kernels, step(): pl.pallas_call(step_kernel, out_shape=shape(((FROM_RIGHT + 1) * ROWS, BLO...  46.1 us
    pallas_call x1, Pallas kernels, adam(): pl.pallas_call(adam_kernel, out_shape=(jax.ShapeDtypeStruct((PARAMS, BLOC...  1.1 us
    unnamed x8, local copies, waits for them, and re-layouts  1.07 us

profile of v6, /device:TPU:1, one launch (start us, length us, event | category | flops | bytes accessed | tf_op | source)
XLA Modules:
  0.0 49.0 jit_solution(15093473185695596359)
XLA Ops:
  0.6 0.0 copy-start.1
  0.6 0.0 copy-start.2
  0.7 0.0 copy-start.3
  0.7 46.1 %render_step.1.grads_ref = f32[1152,128]{1,0:T(8,128)} custom-call(f32[59,1024]{1,0:T(8,128)} %params_ref.1, s32[2,32]{1,0:T(2,128)} %bitcast.7, s32[1,32]{1,0:T(1,128)} %live_hbm.1, s32[1,32]{1,0:T(1,128)} %owner_hbm.1, s32[1,32]{1,0:T(1,128)} %cell_hbm.1, f32[3,8,256]{2,1,0:T(8,128)} %bitcast.6, f32[3]{0:T(128)} %background_hbm.1, ...), custom_call_target="tpu_custom_call" | custom-call | tf_op jit(solution)/shard_map/render_step/pallas_call | solution.py:816
  46.8 0.0 copy-done.1
  46.8 0.0 copy-done.2
  46.8 0.0 copy-done.3
  46.8 0.0 copy-start
  46.8 1.1 %copy-done = f32[1152,128]{1,0:T(8,128)S(1)} copy-done((f32[1152,128]{1,0:T(8,128)S(1)}, f32[1152,128]{1,0:T(8,128)}, u32[]{:S(2)}) %copy-start) | copy-done | bytes 589848
  47.9 1.1 %adam.1 = (f32[59,1024]{1,0:T(8,128)}, f32[59,1024]{1,0:T(8,128)}, f32[59,1024]{1,0:T(8,128)}, f32[59,1024]{1,0:T(8,128)}) custom-call(f32[1152,128]{1,0:T(8,128)S(1)} %copy-done, f32[59,1024]{1,0:T(8,128)S(1)} %copy-done.1, f32[59,1024]{1,0:T(8,128)S(1)} %copy-done.2, f32[59,1024]{1,0:T(8,128)S(1)} %copy-done.3), custom_call_target="tpu_custom_call" | custom-call | tf_op jit(solution)/shard_map/adam/pallas_call | solution.py:896
Async XLA Ops:
  0.6 46.2 %copy-start.1 = (f32[59,1024]{1,0:T(8,128)S(1)}, f32[59,1024]{1,0:T(8,128)}, u32[]{:S(2)}) copy-start(f32[59,1024]{1,0:T(8,128)} %params_ref.1) | copy-start | bytes 724996
  0.6 46.2 %copy-start.2 = (f32[59,1024]{1,0:T(8,128)S(1)}, f32[59,1024]{1,0:T(8,128)}, u32[]{:S(2)}) copy-start(f32[59,1024]{1,0:T(8,128)} %first_ref.1) | copy-start | bytes 724996
  0.7 46.2 %copy-start.3 = (f32[59,1024]{1,0:T(8,128)S(1)}, f32[59,1024]{1,0:T(8,128)}, u32[]{:S(2)}) copy-start(f32[59,1024]{1,0:T(8,128)} %second_ref.1) | copy-start | bytes 724996
  46.8 1.1 %copy-start = (f32[1152,128]{1,0:T(8,128)S(1)}, f32[1152,128]{1,0:T(8,128)}, u32[]{:S(2)}) copy-start(f32[1152,128]{1,0:T(8,128)} %render_step.1.grads_ref) | copy-start | bytes 1769476

commit v7 on v5

--- a/solution.py
+++ b/solution.py
@@ -36,7 +36,7 @@
 LOW = BLOCKS
 HIGH = BLOCKS + 1
 DEAD = POOL
-FROM_LEFT = 2 * SUB
+FROM_LEFT = BLOCKS
 FROM_RIGHT = FROM_LEFT + 1
 ORIGIN_X = 64.0
 ORIGIN_Y = 32.0
@@ -489,12 +489,12 @@
         )
     mean_grads = harmonics_pull(tuple(basis_grads))
     for r in range(10):
-        put_plane(grads_ref, half, r, grads[r] + mean_grads[r] if r < 3 else grads[r])
-    put_plane(grads_ref, half, 10, total * (1.0 - opacity))
+        put_plane(grads_ref, 0, r, grads[r] + mean_grads[r] if r < 3 else grads[r])
+    put_plane(grads_ref, 0, 10, total * (1.0 - opacity))
     for c in range(3):
-        put_plane(grads_ref, half, 11 + 16 * c, tone_grads[c] * harmonic_zero)
+        put_plane(grads_ref, 0, 11 + 16 * c, tone_grads[c] * harmonic_zero)
         for k in range(1, 16):
-            put_plane(grads_ref, half, 11 + 16 * c + k, tone_grads[c] * basis[k - 1])
+            put_plane(grads_ref, 0, 11 + 16 * c + k, tone_grads[c] * basis[k - 1])
 
 
 PARTS = 4 * WIDE // BLOCK
@@ -609,6 +609,7 @@
     cotangent,
     moved,
     summed,
+    cut_grads,
     local_sem,
     halo_send,
     halo_recv,
@@ -733,15 +734,15 @@
     tabulate(0, SUB, pool, stage, turned, table, spread)
     start_all(label)
     got_labels[0] = labels[0]
+    lane = iota((BLOCK, COLS), 1)
+    table[DEAD] = jnp.where(lane == 0, -1e30, 0.0).astype(bf16)
+    spread[DEAD] = jnp.zeros((3, BLOCK, BLOCK), f32)
+
+    for copy in scalars:
+        copy.wait()
     for copy in halo:
         copy.wait_recv()
     tabulate(1, POOL - SUB, pool, stage, turned, table, spread)
-    lane = iota((BLOCK, COLS), 1)
-    table[DEAD] = jnp.where(lane == 0, -1e30, 0.0).astype(bf16)
-    spread[DEAD] = jnp.zeros((3, BLOCK, BLOCK), f32)
-
-    for copy in scalars:
-        copy.wait()
     for h in range(HALVES):
         forward_half(h, blocks, live, features, table, spread, prefix, segment, pieces, alphas)
         rendered = [pieces[r * PIECES : (r + 1) * PIECES, :] for r in range(PARTS)]
@@ -790,10 +791,10 @@
 
     rows = own_block(block_rows[...]).astype(f32)
     gather_moments(rows[0:1], rows[1:2], moved, summed)
-    pull_splat(1, pool, summed, grads_ref)
+    pull_splat(1, pool, summed, cut_grads)
     edges = [
-        remote(block_rows_of(grads_ref, HIGH), block_rows_of(grads_ref, FROM_LEFT), edge_send.at[0], edge_recv.at[0], region=upper),
-        remote(block_rows_of(grads_ref, LOW), block_rows_of(grads_ref, FROM_RIGHT), edge_send.at[1], edge_recv.at[1], region=lower),
+        remote(block_rows_of(cut_grads, HIGH - SUB), block_rows_of(grads_ref, FROM_LEFT), edge_send.at[0], edge_recv.at[0], region=upper),
+        remote(block_rows_of(cut_grads, LOW - SUB), block_rows_of(grads_ref, FROM_RIGHT), edge_send.at[1], edge_recv.at[1], region=lower),
     ]
     for copy in edges:
         copy.start()
@@ -849,6 +850,7 @@
             vmem((WIDE // BLOCK * PIECES * SUB, BLOCK), f32),
             vmem((2 * PIECES * 32, BLOCK), f32),
             vmem((32, 2 * SUB, BLOCK), f32),
+            vmem((SUB * ROWS, BLOCK), f32),
             dma((17,)),
             dma((2,)),
             dma((2,)),

time: 48.4 us -> 48.1 us (level)
  no operation moved by 1% of the time
where the time goes in v7:
time: 48.1 us; the launch traced here: 48 us
  Pallas kernels  46.3 us (96%)
  local copies, waits for them, and re-layouts  0.98 us (2%)
  between operations  0.7 us (1%)
    pallas_call x1, Pallas kernels, step(): pl.pallas_call(step_kernel, out_shape=shape(((FROM_RIGHT + 1) * ROWS, BLO...  45.2 us
    pallas_call x1, Pallas kernels, adam(): pl.pallas_call(adam_kernel, out_shape=(jax.ShapeDtypeStruct((PARAMS, BLOC...  1.1 us
    unnamed x8, local copies, waits for them, and re-layouts  0.98 us

profile of v7, /device:TPU:1, one launch (start us, length us, event | category | flops | bytes accessed | tf_op | source)
XLA Modules:
  0.0 48.0 jit_solution(14374823976833623556)
XLA Ops:
  0.6 0.0 copy-start.1
  0.6 0.0 copy-start.2
  0.7 0.0 copy-start.3
  0.7 45.2 %render_step.1.grads_ref = f32[640,128]{1,0:T(8,128)} custom-call(f32[59,1024]{1,0:T(8,128)} %params_ref.1, s32[2,32]{1,0:T(2,128)} %bitcast.7, s32[1,32]{1,0:T(1,128)} %live_hbm.1, s32[1,32]{1,0:T(1,128)} %owner_hbm.1, s32[1,32]{1,0:T(1,128)} %cell_hbm.1, f32[3,8,256]{2,1,0:T(8,128)} %bitcast.6, f32[3]{0:T(128)} %background_hbm.1, ...), custom_call_target="tpu_custom_call" | custom-call | tf_op jit(solution)/shard_map/render_step/pallas_call | solution.py:817
  45.9 0.0 copy-done.1
  45.9 0.0 copy-done.2
  45.9 0.0 copy-done.3
  45.9 0.0 copy-start
  45.9 1.0 %copy-done = f32[640,128]{1,0:T(8,128)S(1)} copy-done((f32[640,128]{1,0:T(8,128)S(1)}, f32[640,128]{1,0:T(8,128)}, u32[]{:S(2)}) %copy-start) | copy-done | bytes 327704
  46.9 1.1 %adam.1 = (f32[59,1024]{1,0:T(8,128)}, f32[59,1024]{1,0:T(8,128)}, f32[59,1024]{1,0:T(8,128)}, f32[59,1024]{1,0:T(8,128)}) custom-call(f32[640,128]{1,0:T(8,128)S(1)} %copy-done, f32[59,1024]{1,0:T(8,128)S(1)} %copy-done.1, f32[59,1024]{1,0:T(8,128)S(1)} %copy-done.2, f32[59,1024]{1,0:T(8,128)S(1)} %copy-done.3), custom_call_target="tpu_custom_call" | custom-call | tf_op jit(solution)/shard_map/adam/pallas_call | solution.py:898
Async XLA Ops:
  0.6 45.3 %copy-start.1 = (f32[59,1024]{1,0:T(8,128)S(1)}, f32[59,1024]{1,0:T(8,128)}, u32[]{:S(2)}) copy-start(f32[59,1024]{1,0:T(8,128)} %params_ref.1) | copy-start | bytes 724996
  0.6 45.3 %copy-start.2 = (f32[59,1024]{1,0:T(8,128)S(1)}, f32[59,1024]{1,0:T(8,128)}, u32[]{:S(2)}) copy-start(f32[59,1024]{1,0:T(8,128)} %first_ref.1) | copy-start | bytes 724996
  0.7 45.3 %copy-start.3 = (f32[59,1024]{1,0:T(8,128)S(1)}, f32[59,1024]{1,0:T(8,128)}, u32[]{:S(2)}) copy-start(f32[59,1024]{1,0:T(8,128)} %second_ref.1) | copy-start | bytes 724996
  45.9 1.0 %copy-start = (f32[640,128]{1,0:T(8,128)S(1)}, f32[640,128]{1,0:T(8,128)}, u32[]{:S(2)}) copy-start(f32[640,128]{1,0:T(8,128)} %render_step.1.grads_ref) | copy-start | bytes 983044
